TPU v7x, 256 devices: a whole 4x4x8 slice. The times are simulated.
256 devices in a mesh: dp: 2 (over z_lo), station: 8 (over y, core), tm: 16 (over z_hi, x).
Axes of the slice: x: 4, y: 4, z: 8 (z_hi: 4, z_lo: 2; z = z_hi * 2 + z_lo), core: 2. Of those that a mesh axis runs over, the one named last changes fastest.
Arguments:
- inputs: bfloat16 [2, 256, 256, 512], P('dp', 'station', 'tm'), may hold values from -6 to 6
- cotangent: bfloat16 [2, 256, 256, 512], P('dp', 'station', 'tm'), may hold values from -6 to 6
- station_gain: float32 [512], replicated, may hold values from 0.5 to 1.5
- station_qkv: bfloat16 [512, 1536], replicated, may hold values from -0.25 to 0.25
- station_out: bfloat16 [512, 512], replicated, may hold values from -0.25 to 0.25
- time_gain: float32 [512], replicated, may hold values from 0.5 to 1.5
- time_qkv: bfloat16 [512, 1536], replicated, may hold values from -0.25 to 0.25
- time_out: bfloat16 [512, 512], replicated, may hold values from -0.25 to 0.25
Outputs:
- grad_inputs: bfloat16 [2, 256, 256, 512], P('dp', 'station', 'tm')
- grad_station_qkv: bfloat16 [512, 1536], P('station', 'tm')
- grad_station_out: bfloat16 [512, 512], P('station', 'tm')
- grad_station_gain: float32 [512], replicated
- grad_time_qkv: bfloat16 [512, 1536], P('station', 'tm')
- grad_time_out: bfloat16 [512, 512], P('station', 'tm')
- grad_time_gain: float32 [512], replicated
All inputs are finite; a program needn't handle non-finite values.
Results may differ from a plain program's by a relative error of at most 0.03.
Values may be sent and summed in bfloat16 or wider, within the bound.
A program may use at most 128 MiB of HBM per device.

v0:
```python
import jax
import jax.numpy as jnp
from jax import lax
from jax.sharding import PartitionSpec as P

HEADS = 8


EPSILON = 1e-05


def layer_parts(inputs, gains, w_qkv):
    groups, length, inner, width = inputs.shape
    heads_dim = width // HEADS
    head_shape = (groups, length, inner, HEADS, heads_dim)
    rows_full = inputs.reshape(groups * length * inner, width).astype(jnp.float32)
    inverse = lax.rsqrt(jnp.mean(rows_full * rows_full, axis=1, keepdims=True) + EPSILON)
    normed = rows_full * inverse
    acted = (normed * gains).astype(jnp.bfloat16)
    joined = jnp.dot(acted, w_qkv, preferred_element_type=jnp.float32).astype(jnp.bfloat16)
    queries = joined[:, :width].reshape(head_shape)
    keys_part = joined[:, width : 2 * width].reshape(head_shape)
    values_part = joined[:, 2 * width :].reshape(head_shape)
    scale = heads_dim ** (-0.5)
    scores = (
        jnp.einsum("alche,amche->achlm", queries, keys_part, preferred_element_type=jnp.float32)
        * scale
    )
    expon = jnp.exp(scores)
    weights_full = expon / jnp.sum(expon, axis=-1, keepdims=True)
    weights_half = weights_full.astype(jnp.bfloat16)
    attended = (
        jnp.einsum(
            "achlm,amche->alche", weights_half, values_part, preferred_element_type=jnp.float32
        )
        .astype(jnp.bfloat16)
        .reshape(-1, width)
    )
    return (
        rows_full,
        inverse,
        normed,
        acted,
        queries,
        keys_part,
        values_part,
        weights_full,
        weights_half,
        attended,
    )


def layer_forward(inputs, gains, w_qkv, w_out):
    parts = layer_parts(inputs, gains, w_qkv)
    result = (
        (parts[0] + jnp.dot(parts[9], w_out, preferred_element_type=jnp.float32))
        .astype(jnp.bfloat16)
        .reshape(inputs.shape)
    )
    return (result, parts)


def backward_from(parts, shape, upstream, gains, w_qkv, w_out):
    (
        rows_full,
        inverse,
        normed,
        acted,
        queries,
        keys_part,
        values_part,
        weights_full,
        weights_half,
        attended,
    ) = parts
    width = shape[3]
    head_shape = queries.shape
    scale = head_shape[4] ** (-0.5)
    up_rows = upstream.reshape(-1, width)
    grad_out = lax.dot_general(
        attended, up_rows, (((0,), (0,)), ((), ())), preferred_element_type=jnp.float32
    )
    grad_att = (
        lax.dot_general(
            up_rows, w_out, (((1,), (1,)), ((), ())), preferred_element_type=jnp.float32
        )
        .astype(jnp.bfloat16)
        .reshape(head_shape)
    )
    grad_weights = jnp.einsum(
        "alche,amche->achlm", grad_att, values_part, preferred_element_type=jnp.float32
    )
    grad_values = jnp.einsum(
        "achlm,alche->amche", weights_half, grad_att, preferred_element_type=jnp.float32
    ).astype(jnp.bfloat16)
    row_dot = jnp.sum(grad_weights * weights_full, axis=-1, keepdims=True)
    grad_scores = (weights_full * (grad_weights - row_dot) * scale).astype(jnp.bfloat16)
    grad_queries = jnp.einsum(
        "achlm,amche->alche", grad_scores, keys_part, preferred_element_type=jnp.float32
    ).astype(jnp.bfloat16)
    grad_keys = jnp.einsum(
        "achlm,alche->amche", grad_scores, queries, preferred_element_type=jnp.float32
    ).astype(jnp.bfloat16)
    grad_joined = jnp.concatenate(
        [
            grad_queries.reshape(-1, width),
            grad_keys.reshape(-1, width),
            grad_values.reshape(-1, width),
        ],
        axis=1,
    )
    grad_qkv = lax.dot_general(
        acted, grad_joined, (((0,), (0,)), ((), ())), preferred_element_type=jnp.float32
    )
    grad_acted = lax.dot_general(
        grad_joined, w_qkv, (((1,), (1,)), ((), ())), preferred_element_type=jnp.float32
    )
    grad_gain = jnp.sum(grad_acted * normed, axis=0)
    grad_normed = grad_acted * gains
    grad_rows = inverse * (
        grad_normed - normed * jnp.mean(grad_normed * normed, axis=1, keepdims=True)
    )
    grad_inputs = (up_rows.astype(jnp.float32) + grad_rows).astype(jnp.bfloat16).reshape(shape)
    return (grad_inputs, grad_qkv, grad_out, grad_gain)


def layer_backward(inputs, upstream, gains, w_qkv, w_out):
    return backward_from(
        layer_parts(inputs, gains, w_qkv), inputs.shape, upstream, gains, w_qkv, w_out
    )


def reduce_weights(first_grad, second_grad):
    columns = (
        lax.psum_scatter(
            first_grad.astype(jnp.bfloat16), "tm", scatter_dimension=1, tiled=True
        ).astype(jnp.float32),
        lax.psum_scatter(
            second_grad.astype(jnp.bfloat16), "tm", scatter_dimension=1, tiled=True
        ).astype(jnp.float32),
    )
    rows_part = (
        lax.psum_scatter(
            columns[0].astype(jnp.bfloat16), "station", scatter_dimension=0, tiled=True
        ).astype(jnp.float32),
        lax.psum_scatter(
            columns[1].astype(jnp.bfloat16), "station", scatter_dimension=0, tiled=True
        ).astype(jnp.float32),
    )
    totals = (
        lax.psum(rows_part[0].astype(jnp.bfloat16), "dp").astype(jnp.float32),
        lax.psum(rows_part[1].astype(jnp.bfloat16), "dp").astype(jnp.float32),
    )
    return (totals[0].astype(jnp.bfloat16), totals[1].astype(jnp.bfloat16))


def local(inputs, cotangent, station_gain, station_qkv, station_out, time_gain, time_qkv, time_out):
    station_view = lax.all_to_all(inputs, "station", split_axis=2, concat_axis=1, tiled=True)
    mid_station, station_parts = layer_forward(station_view, station_gain, station_qkv, station_out)
    mid_time = lax.all_to_all(
        lax.all_to_all(mid_station, "station", split_axis=1, concat_axis=2, tiled=True),
        "tm",
        split_axis=1,
        concat_axis=2,
        tiled=True,
    )
    up_time = lax.all_to_all(cotangent, "tm", split_axis=1, concat_axis=2, tiled=True)
    first, second, epochs, width = mid_time.shape
    grad_mid, time_qkv_part, time_out_part, time_gain_part = layer_backward(
        mid_time.reshape(first * second, epochs, 1, width),
        up_time.reshape(first * second, epochs, 1, width),
        time_gain,
        time_qkv,
        time_out,
    )
    grad_mid = grad_mid.reshape(first, second, epochs, width)
    grad_station_view = lax.all_to_all(
        lax.all_to_all(grad_mid, "tm", split_axis=2, concat_axis=1, tiled=True),
        "station",
        split_axis=2,
        concat_axis=1,
        tiled=True,
    )
    grad_station, station_qkv_part, station_out_part, station_gain_part = backward_from(
        station_parts, station_view.shape, grad_station_view, station_gain, station_qkv, station_out
    )
    grad_inputs = lax.all_to_all(grad_station, "station", split_axis=1, concat_axis=2, tiled=True)
    time_sums = reduce_weights(time_qkv_part, time_out_part)
    station_sums = reduce_weights(station_qkv_part, station_out_part)
    gain_totals = lax.psum((station_gain_part, time_gain_part), ("dp", "station", "tm"))
    return (
        grad_inputs,
        station_sums[0],
        station_sums[1],
        gain_totals[0],
        time_sums[0],
        time_sums[1],
        gain_totals[1],
    )


def solution(mesh):
    in_specs = (
        P("dp", "station", "tm", None),
        P("dp", "station", "tm", None),
        P(),
        P(),
        P(),
        P(),
        P(),
        P(),
    )
    out_specs = (
        P("dp", "station", "tm", None),
        P("station", "tm"),
        P("station", "tm"),
        P(),
        P("station", "tm"),
        P("station", "tm"),
        P(),
    )
    return jax.shard_map(local, mesh=mesh, in_specs=in_specs, out_specs=out_specs, check_vma=False)
```

profile of v0, /device:TPU:6, one launch (start us, length us, event | category | flops | bytes accessed | tf_op | source)
XLA Modules:
  0.0 691.1 jit_solution(12937538542856233094)
XLA Ops:
  8.7 14.7 %all_to_all.102 = bf16[1,32,16,512]{3,1,0,2:T(8,128)(2,1)S(1)} all-to-all(bf16[1,32,16,512]{3,1,0,2:T(8,128)(2,1)S(1)} %copy.144), channel_id=1, replica_groups=mesh['dp'=2,'station'=8,'tm'=16] {'station'}, dimensions={2} | all-to-all | bytes 1048576 | tf_op jit(solution)/shard_map/all_to_all | solution.py:158
  58.1 14.5 %all_to_all.103 = bf16[1,256,2,512]{3,2,0,1:T(2,128)(2,1)} all-to-all(bf16[1,256,2,512]{3,2,0,1:T(2,128)(2,1)} %bitcast.161), channel_id=1, replica_groups=mesh['dp'=2,'station'=8,'tm'=16] {'station'}, dimensions={1} | all-to-all | bytes 1048576 | tf_op jit(solution)/shard_map/all_to_all | solution.py:161
  72.6 11.4 %all-to-all-start = ((bf16[1,32,16,512]{3,2,0,1:T(8,128)(2,1)}), bf16[1,32,16,512]{3,2,0,1:T(8,128)(2,1)}, u32[]{:S(2)}, u32[]{:S(2)}) async-start(bf16[1,32,16,512]{3,2,0,1:T(8,128)(2,1)} %bitcast.172), calls=%async_computation | async-start | bytes 1048576 | tf_op jit(solution)/shard_map/all_to_all | solution.py:167
  86.3 13.3 %all-to-all-done = bf16[1,32,16,512]{3,2,0,1:T(8,128)(2,1)} async-done(((bf16[1,32,16,512]{3,2,0,1:T(8,128)(2,1)}), bf16[1,32,16,512]{3,2,0,1:T(8,128)(2,1)}, u32[]{:S(2)}, u32[]{:S(2)}) %all-to-all-start) | async-done | bytes 524320 | tf_op jit(solution)/shard_map/all_to_all | solution.py:167
  99.6 6.9 all-to-all-start.3
  114.7 6.5 all-to-all-done.3
  142.0 4.0 fusion.83
  150.6 9.0 %fusion.45 = bf16[2,256,1,8,64]{1,4,3,0,2:T(8,128)(2,1)} fusion(bf16[2,256,8,64]{1,3,2,0:T(8,128)(2,1)} %copy.163, f32[2,8,256,256]{2,3,1,0:T(8,128)} %fusion.83, f32[2,8,256,256]{2,3,1,0:T(8,128)} %copy-done.7, f32[2,8,256]{2,1,0:T(8,128)S(1)} %get-tuple-element.53), kind=kOutput, calls=%fused_computation.44 | convolution fusion | flops 143921408 | bytes 9453568 | tf_op jit(solution)/shard_map/achlm,alche->amche/dot_general | solution.py:101
  159.6 8.9 %fusion.48 = bf16[2,256,1,8,64]{1,4,3,0,2:T(8,128)(2,1)} fusion(bf16[2,256,8,64]{1,3,2,0:T(8,128)(2,1)} %copy.169, f32[2,8,256,256]{2,3,1,0:T(8,128)} %fusion.83, f32[2,8,256,256]{2,3,1,0:T(8,128)} %copy-done.7, f32[2,8,256]{2,1,0:T(8,128)S(1)} %get-tuple-element.53), kind=kOutput, calls=%fused_computation.45 | convolution fusion | flops 143921408 | bytes 9453568 | tf_op jit(solution)/shard_map/achlm,amche->alche/dot_general | solution.py:98
  175.7 6.6 all-to-all-start.4
  187.8 8.6 %all-to-all-done.4 = bf16[1,2,256,512]{3,1,0,2:T(2,128)(2,1)S(1)} async-done(((bf16[1,2,256,512]{3,1,0,2:T(2,128)(2,1)}), bf16[1,2,256,512]{3,1,0,2:T(2,128)(2,1)S(1)}, u32[]{:S(2)}, u32[]{:S(2)}) %all-to-all-start.4) | async-done | bytes 524320 | tf_op jit(solution)/shard_map/all_to_all | solution.py:178
  196.8 13.9 %all_to_all.104 = bf16[1,32,16,512]{3,1,0,2:T(8,128)(2,1)S(1)} all-to-all(bf16[1,32,16,512]{3,1,0,2:T(8,128)(2,1)S(1)} %copy.181), channel_id=1, replica_groups=mesh['dp'=2,'station'=8,'tm'=16] {'station'}, dimensions={2} | all-to-all | bytes 1048576 | tf_op jit(solution)/shard_map/all_to_all | solution.py:177
  219.5 4.1 fusion.43
  230.7 9.0 %fusion.51 = bf16[1,256,2,8,64]{1,4,3,2,0:T(8,128)(2,1)} fusion(bf16[256,2,8,64]{0,3,2,1:T(8,128)(2,1)} %copy.149, f32[2,8,256,256]{2,3,1,0:T(8,128)} %fusion.84, f32[2,8,256,256]{2,3,1,0:T(8,128)} %copy-done.6, f32[2,8,256]{2,1,0:T(8,128)S(1)} %get-tuple-element.51), kind=kOutput, calls=%fused_computation.46 | convolution fusion | flops 143921408 | bytes 9453568 | tf_op jit(solution)/shard_map/achlm,alche->amche/dot_general | solution.py:101
  243.1 8.7 %fusion.54 = bf16[1,256,2,8,64]{1,4,3,2,0:T(8,128)(2,1)} fusion(bf16[256,2,8,64]{0,3,2,1:T(8,128)(2,1)S(1)} %copy-done.10, f32[2,8,256,256]{2,3,1,0:T(8,128)} %fusion.84, f32[2,8,256,256]{2,3,1,0:T(8,128)} %copy-done.6, f32[2,8,256]{2,1,0:T(8,128)S(1)} %get-tuple-element.51), kind=kOutput, calls=%fused_computation.47 | convolution fusion | flops 143921408 | bytes 9453568 | tf_op jit(solution)/shard_map/achlm,amche->alche/dot_general | solution.py:98
  261.1 10.8 %reduce-scatter.23.cloned.1.call-done = bf16[512,32]{0,1:T(8,128)(2,1)} async-done(((bf16[512,512]{0,1:T(8,128)(2,1)}), bf16[512,32]{0,1:T(8,128)(2,1)}) %reduce-scatter.23.cloned.1.call-update) | async-done | bytes 32784 | tf_op jit(solution)/shard_map/reduce_scatter | solution.py:138
  279.2 4.3 all-to-all-start.6
  283.6 75.6 %reduce-scatter.19.cloned.1.call-done = bf16[512,32]{0,1:T(8,128)(2,1)} async-done(((bf16[512,512]{0,1:T(8,128)(2,1)}), bf16[512,32]{0,1:T(8,128)(2,1)}) %reduce-scatter.19.cloned.1.call-update) | async-done | bytes 32784 | tf_op jit(solution)/shard_map/reduce_scatter | solution.py:138
  360.8 86.8 %reduce-scatter.21.cloned.1.call-done = bf16[512,96]{0,1:T(8,128)(2,1)} async-done(((bf16[512,1536]{0,1:T(8,128)(2,1)}), bf16[512,96]{0,1:T(8,128)(2,1)}) %reduce-scatter.21.cloned.1.call-update) | async-done | bytes 98320 | tf_op jit(solution)/shard_map/reduce_scatter | solution.py:135
  449.3 86.4 %reduce-scatter.17.cloned.1.call-done = bf16[512,96]{0,1:T(8,128)(2,1)} async-done(((bf16[512,1536]{0,1:T(8,128)(2,1)}), bf16[512,96]{0,1:T(8,128)(2,1)}) %reduce-scatter.17.cloned.1.call-update) | async-done | bytes 98320 | tf_op jit(solution)/shard_map/reduce_scatter | solution.py:135
  537.4 32.0 %reduce-scatter.31.cloned.1.call-done = bf16[64,32]{1,0:T(8,128)(2,1)} async-done(((bf16[512,32]{1,0:T(8,128)(2,1)}), bf16[64,32]{1,0:T(8,128)(2,1)}) %reduce-scatter.31.cloned.1.call-update) | async-done | bytes 4112
  570.2 74.1 %all-reduce = (f32[512]{0:T(512)}, f32[512]{0:T(512)}) all-reduce(f32[512]{0:T(512)S(1)} %get-tuple-element.37, f32[512]{0:T(512)S(1)} %get-tuple-element.35), channel_id=1, replica_groups=mesh['dp'=2,'station'=8,'tm'=16] {'dp','station','tm'}, use_global_device_ids=true, to_apply=%region_15.0 | all-reduce | flops 1024 | bytes 8192 | tf_op jit(solution)/shard_map/psum | solution.py:190
  647.4 24.9 %reduce-scatter.25.cloned.1.call-done = bf16[64,96]{1,0:T(8,128)(2,1)} async-done(((bf16[512,96]{1,0:T(8,128)(2,1)}), bf16[64,96]{1,0:T(8,128)(2,1)}) %reduce-scatter.25.cloned.1.call-update) | async-done | bytes 12304
  673.2 9.5 %all-reduce.1 = (bf16[64,96]{0,1:T(8,128)(2,1)S(1)}, bf16[64,32]{0,1:T(8,128)(2,1)}, bf16[64,96]{0,1:T(8,128)(2,1)S(1)}, bf16[64,32]{0,1:T(8,128)(2,1)}) all-reduce(bf16[64,96]{0,1:T(8,128)(2,1)S(1)} %copy.210, bf16[64,32]{0,1:T(8,128)(2,1)S(1)} %copy.212, ...), channel_id=1, replica_groups=mesh['dp'=2,'station'=8,'tm'=16] {'dp'}, use_global_device_ids=true, to_apply=%region_10.0 | all-reduce | flops 16384 | bytes 65536 | tf_op jit(solution)/shard_map/psum | solution.py:151
  (170 shorter events, 131.7 us)
Async XLA Ops:
  7.2 117.9 %copy-start = (bf16[512,1536]{1,0:T(8,128)(2,1)S(1)}, bf16[512,1536]{1,0:T(8,128)(2,1)}, u32[]{:S(2)}) copy-start(bf16[512,1536]{1,0:T(8,128)(2,1)} %param.14) | copy-start | bytes 4718596
  7.2 20.2 %copy-start.23 = (f32[512]{0:T(512)S(1)}, f32[512]{0:T(512)}, u32[]{:S(2)}) copy-start(f32[512]{0:T(512)} %param.10) | copy-start | bytes 6148
  34.5 12.5 %copy-start.9 = (bf16[256,2,8,64]{0,3,2,1:T(8,128)(2,1)}, bf16[256,2,8,64]{0,3,2,1:T(8,128)(2,1)S(1)}, u32[]{:S(2)}) copy-start(bf16[256,2,8,64]{0,3,2,1:T(8,128)(2,1)S(1)} %copy.150) | copy-start | bytes 1572868
  53.6 32.7 %copy-start.4 = (bf16[512,512]{1,0:T(8,128)(2,1)}, bf16[512,512]{1,0:T(8,128)(2,1)S(1)}, u32[]{:S(2)}) copy-start(bf16[512,512]{1,0:T(8,128)(2,1)S(1)} %reshape.243) | copy-start | bytes 1572868
  72.6 26.9 %all-to-all-start = ((bf16[1,32,16,512]{3,2,0,1:T(8,128)(2,1)}), bf16[1,32,16,512]{3,2,0,1:T(8,128)(2,1)}, u32[]{:S(2)}, u32[]{:S(2)}) async-start(bf16[1,32,16,512]{3,2,0,1:T(8,128)(2,1)} %bitcast.172), calls=%async_computation | async-start | bytes 1048576 | tf_op jit(solution)/shard_map/all_to_all | solution.py:167
  99.6 21.6 %all-to-all-start.3 = ((bf16[1,32,16,512]{3,2,0,1:T(8,128)(2,1)}), bf16[1,32,16,512]{3,2,0,1:T(8,128)(2,1)}, u32[]{:S(2)}, u32[]{:S(2)}) async-start(bf16[1,32,16,512]{3,2,0,1:T(8,128)(2,1)} %copy.157), calls=%async_computation.3 | async-start | bytes 1048576 | tf_op jit(solution)/shard_map/all_to_all | solution.py:160
  107.5 17.4 %copy-start.22 = (f32[512]{0:T(512)S(1)}, f32[512]{0:T(512)}, u32[]{:S(2)}) copy-start(f32[512]{0:T(512)} %param.13) | copy-start | bytes 6148
  142.0 6.9 %copy-start.14 = (bf16[2,256,8,64]{1,3,2,0:T(8,128)(2,1)S(1)}, bf16[2,256,8,64]{1,3,2,0:T(8,128)(2,1)}, u32[]{:S(2)}) copy-start(bf16[2,256,8,64]{1,3,2,0:T(8,128)(2,1)} %copy.167) | copy-start | bytes 1572868
  174.0 8.8 %copy-start.13 = (bf16[2,256,8,64]{1,3,2,0:T(8,128)(2,1)S(1)}, bf16[2,256,8,64]{1,3,2,0:T(8,128)(2,1)}, u32[]{:S(2)}) copy-start(bf16[2,256,8,64]{1,3,2,0:T(8,128)(2,1)} %copy.168) | copy-start | bytes 1572868
  175.7 20.8 %all-to-all-start.4 = ((bf16[1,2,256,512]{3,1,0,2:T(2,128)(2,1)}), bf16[1,2,256,512]{3,1,0,2:T(2,128)(2,1)S(1)}, u32[]{:S(2)}, u32[]{:S(2)}) async-start(bf16[1,2,256,512]{3,1,0,2:T(2,128)(2,1)} %copy.178), calls=%async_computation.4 | async-start | bytes 1048576 | tf_op jit(solution)/shard_map/all_to_all | solution.py:178
  182.3 89.7 %reduce-scatter.23.cloned.1.call-start = ((), (), s32[]{:S(2)}) async-start(), calls=%async_computation.18 | async-start | bytes 557056 | tf_op jit(solution)/shard_map/reduce_scatter | solution.py:138
  186.4 25.1 %copy-start.5 = (bf16[512,512]{1,0:T(8,128)(2,1)S(1)}, bf16[512,512]{1,0:T(8,128)(2,1)}, u32[]{:S(2)}) copy-start(bf16[512,512]{1,0:T(8,128)(2,1)} %copy-done.4) | copy-start | bytes 1572868
  187.7 171.4 %reduce-scatter.19.cloned.1.call-start = ((), (), s32[]{:S(2)}) async-start(), calls=%async_computation.16 | async-start | bytes 557056 | tf_op jit(solution)/shard_map/reduce_scatter | solution.py:138
  212.8 234.7 %reduce-scatter.21.cloned.1.call-start = ((), (), s32[]{:S(2)}) async-start(), calls=%async_computation.17 | async-start | bytes 1671168 | tf_op jit(solution)/shard_map/reduce_scatter | solution.py:135
  216.7 319.0 %reduce-scatter.17.cloned.1.call-start = ((), (), s32[]{:S(2)}) async-start(), calls=%async_computation.15 | async-start | bytes 1671168 | tf_op jit(solution)/shard_map/reduce_scatter | solution.py:135
  219.5 7.5 %copy-start.12 = (bf16[256,2,8,64]{0,3,2,1:T(8,128)(2,1)S(1)}, bf16[256,2,8,64]{0,3,2,1:T(8,128)(2,1)}, u32[]{:S(2)}) copy-start(bf16[256,2,8,64]{0,3,2,1:T(8,128)(2,1)} %copy.151) | copy-start | bytes 1572868
  230.7 12.4 %copy-start.10 = (bf16[256,2,8,64]{0,3,2,1:T(8,128)(2,1)S(1)}, bf16[256,2,8,64]{0,3,2,1:T(8,128)(2,1)}, u32[]{:S(2)}) copy-start(bf16[256,2,8,64]{0,3,2,1:T(8,128)(2,1)} %copy-done.9) | copy-start | bytes 1572868
  258.6 14.9 %copy-start.24 = (bf16[512,1536]{1,0:T(8,128)(2,1)S(1)}, bf16[512,1536]{1,0:T(8,128)(2,1)}, u32[]{:S(2)}) copy-start(bf16[512,1536]{1,0:T(8,128)(2,1)} %param.11) | copy-start | bytes 4718596
  261.1 308.3 %reduce-scatter.31.cloned.1.call-start = ((), (), s32[]{:S(2)}) async-start(), calls=%async_computation.22 | async-start | bytes 147456
  276.1 408.1 %copy-start.1 = (bf16[512,1536]{1,0:T(8,128)(2,1)S(1)}, bf16[512,1536]{1,0:T(8,128)(2,1)}, u32[]{:S(2)}) copy-start(bf16[512,1536]{1,0:T(8,128)(2,1)} %param.14) | copy-start | bytes 4718596
  279.2 365.0 %all-to-all-start.6 = ((bf16[1,256,2,512]{3,2,0,1:T(2,128)(2,1)}), bf16[1,256,2,512]{3,2,0,1:T(2,128)(2,1)S(1)}, u32[]{:S(2)}, u32[]{:S(2)}) async-start(bf16[1,256,2,512]{3,2,0,1:T(2,128)(2,1)} %bitcast.39), calls=%async_computation.6 | async-start | bytes 1048576 | tf_op jit(solution)/shard_map/all_to_all | solution.py:187
  283.5 362.3 %reduce-scatter.27.cloned.1.call-start = ((), (), s32[]{:S(2)}) async-start(), calls=%async_computation.20 | async-start | bytes 147456
  360.7 285.9 %reduce-scatter.29.cloned.1.call-start = ((), (), s32[]{:S(2)}) async-start(), calls=%async_computation.21 | async-start | bytes 147456
  449.3 223.1 %reduce-scatter.25.cloned.1.call-start = ((), (), s32[]{:S(2)}) async-start(), calls=%async_computation.19 | async-start | bytes 147456
  (13 other events, 37.3 us)
Sparse Core Ops, SparseCore 0:
  187.9 84.0 reduce-scatter.22
  275.8 83.3 reduce-scatter.18
  362.7 84.8 reduce-scatter.20
  450.9 84.7 reduce-scatter.16
  538.0 31.2 reduce-scatter.30
  571.9 31.9 reduce-scatter.26
  606.3 31.5 reduce-scatter.28
  640.6 31.7 reduce-scatter.24
where the time goes:
time: 702 us; the launch traced here: 691 us
  waiting for transfers between devices  345 us (49%)
  blocking collectives  127 us (18%)
  local copies, waits for them, and re-layouts  93.1 us (13%)
  matrix products  77.2 us (11%)
  starting transfers between devices  29.9 us (4%)
  between operations  14.9 us (2%)
    reduce_scatter x2, waiting for transfers between devices, reduce_weights(): lax.psum_scatter(first_grad.astype(jnp.bfloat16), 'tm', scatter_dimension...  173 us
    reduce_scatter x2, waiting for transfers between devices, reduce_weights(): lax.psum_scatter(second_grad.astype(jnp.bfloat16), 'tm', scatter_dimensio...  86.4 us
    psum x1, blocking collectives, local(): lax.psum((station_gain_part, time_gain_part), ('dp', 'station', 'tm'))  74.1 us
    unnamed x12, waiting for transfers between devices  57.1 us
    another operation x16, local copies, waits for them, and re-layouts  35.8 us
    unnamed x70, local copies, waits for them, and re-layouts  21.2 us
    dot_general x2, matrix products, backward_from(): jnp.einsum('achlm,alche->amche', grad_scores, queries, preferred_element_...  17.9 us
    dot_general x2, matrix products, backward_from(): jnp.einsum('achlm,amche->alche', grad_scores, keys_part, preferred_elemen...  17.6 us
  transfers between devices with their start and end apart: 12, of which 9 were waited for; matrix products, arithmetic and copies ran while one was open for 12% of the time, Pallas kernels for 0%

commit v1 on v0

v1 whole, which is shorter than its diff:
```python
import functools

import jax
import jax.numpy as jnp
from jax import lax
from jax.experimental import pallas as pl
from jax.experimental.pallas import tpu as pltpu
from jax.sharding import PartitionSpec as P

MESH = pl.DeviceIdType.MESH
BF = jnp.bfloat16
F32 = jnp.float32
EPSILON = 1e-05
WIDTH = 512
TOKENS = 512
SEQ = 256
PAIRS = 4
PEERS = 128

R_IN, R_COT, R_MID, R_GMID, R_GIN, R_GAIN_S, R_GAIN_X, R_GAIN_Z, R_TIME, R_STATION = (
    0, 1, 2, 3, 4, 5, 6, 7, 8, 12,
)
N_SEMS = 16
L_X, L_COT, L_WQS, L_WOS, L_WQT, L_WOT = range(6)


def nn(a, b):
    return jnp.dot(a, b, preferred_element_type=F32)


def nt(a, b):
    return lax.dot_general(a, b, (((1,), (1,)), ((), ())), preferred_element_type=F32)


def columns(pair, base=0):
    return pl.ds(pl.multiple_of(base + pair * 128, 128), 128)


def half_masks(value):
    lane = lax.broadcasted_iota(jnp.int32, (1, 128), 1)
    first = jnp.where(lane < 64, value, 0.0).astype(BF)
    second = jnp.where(lane < 64, 0.0, value).astype(BF)
    return first, second


def normalise(x, gain):
    inverse = lax.rsqrt(jnp.mean(x * x, axis=1, keepdims=True) + EPSILON)
    normed = x * inverse
    return inverse, (normed * gain).astype(BF)


def softmax_t(scores):
    expon = jnp.exp(scores)
    total = jnp.sum(expon, axis=0, keepdims=True)
    shrink = jnp.where(total > 1.0, 0.25, 1.0)
    return (expon * shrink) * (1.0 / (total * shrink))


def forward_step(step, joined, probs, att_t):
    seq, pair = step // PAIRS, lax.rem(step, PAIRS)
    rows = pl.ds(pl.multiple_of(seq * SEQ, SEQ), SEQ)
    queries = joined[rows, columns(pair)]
    keys = joined[rows, columns(pair, WIDTH)]
    values_t = joined[rows, columns(pair, 2 * WIDTH)].T
    masks = half_masks(0.125)
    for head in range(2):
        p = softmax_t(nt(keys, queries * masks[head]))
        probs[2 * step + head] = p
        out = nn(values_t[64 * head : 64 * head + 64], p.astype(BF)).astype(BF)
        att_t[pl.ds(pl.multiple_of(pair * 128 + 64 * head, 64), 64), rows] = out


def backward_step(step, joined, probs, att_t, grad_att, grad_joined, grad_q_t, forward):
    seq, pair = step // PAIRS, lax.rem(step, PAIRS)
    rows = pl.ds(pl.multiple_of(seq * SEQ, SEQ), SEQ)
    queries = joined[rows, columns(pair)]
    keys = joined[rows, columns(pair, WIDTH)]
    values = joined[rows, columns(pair, 2 * WIDTH)]
    upstream = grad_att[rows, columns(pair)]
    eighths = half_masks(0.125)
    ones = half_masks(1.0)
    keys_t = (keys * jnp.asarray(0.125, BF)).T
    if forward:
        values_t = values.T
    qs, us, p_halves, grad_ss = [], [], [], []
    for head in range(2):
        half = slice(64 * head, 64 * head + 64)
        q = queries * eighths[head]
        u = upstream * ones[head]
        if forward:
            p = softmax_t(nt(keys, q))
        else:
            p = probs[2 * step + head]
        p_half = p.astype(BF)
        out_rows = pl.ds(pl.multiple_of(pair * 128 + 64 * head, 64), 64)
        if forward:
            att_t[out_rows, rows] = nn(values_t[half], p_half).astype(BF)
        grad_p = nt(values, u)
        dot = jnp.sum(grad_p * p, axis=0, keepdims=True)
        grad_s = (p * (grad_p - dot)).astype(BF)
        grad_q_t[out_rows, rows] = nn(keys_t[half], grad_s).astype(BF)
        qs.append(q)
        us.append(u)
        p_halves.append(p_half)
        grad_ss.append(grad_s)
    grad_k = nn(jnp.concatenate(grad_ss, axis=1), jnp.concatenate(qs, axis=0))
    grad_v = nn(jnp.concatenate(p_halves, axis=1), jnp.concatenate(us, axis=0))
    grad_joined[rows, columns(pair, WIDTH)] = grad_k.astype(BF)
    grad_joined[rows, columns(pair, 2 * WIDTH)] = grad_v.astype(BF)


def norm_backward(x, inverse, gain, grad_acted, upstream):
    normed = x * inverse
    grad_gain = jnp.sum(grad_acted * normed, axis=0, keepdims=True)
    grad_normed = grad_acted * gain
    mean = jnp.mean(grad_normed * normed, axis=1, keepdims=True)
    return grad_gain, upstream + inverse * (grad_normed - normed * mean)


def pack(block_of, wide, send):
    for k in range(4):
        block = block_of(k)
        for c in range(4):
            wide[pl.ds(c * 4 + k, PEERS, stride=16), :] = block[:, 128 * c : 128 * c + 128]
    send[...] = wide[...].astype(BF).reshape(PEERS, 16, 128)


def unpack(recv, wide, store):
    wide[...] = recv[...].reshape(PEERS * 16, 128).astype(F32)
    for k in range(4):
        for c in range(4):
            store(k, c, wide[pl.ds(c * 4 + k, PEERS, stride=16), :])


def kernel(
    x_hbm, cot_hbm, gain_s_ref, wq_s_hbm, wo_s_hbm, gain_t_ref, wq_t_hbm, wo_t_hbm,
    gin_ref, gq_s_ref, go_s_ref, gg_s_ref, gq_t_ref, go_t_ref, gg_t_ref,
    x_raw, fine, wide, in_send, xs, cot_recv, ups_t, wq_s, wo_s, wq_t, wo_t,
    acted, joined_s, joined_t, probs, att_t, grad_att, grad_joined, grad_q_t, acted_t,
    mid_send, mid_recv, xt, gmid_send, gmid_recv, ups_s, gin_send, gin_recv,
    total, pair_send, pair_recv, y_send, y_recv, x_send, x_recv, z_send, z_recv,
    gain_send, gain_s_recv, gain_x_recv, gain_z_recv,
    send_sems, recv_sems, local_sems,
):
    dp, station, tm = lax.axis_index("dp"), lax.axis_index("station"), lax.axis_index("tm")
    me = station * 16 + tm
    y, core = station // 2, lax.rem(station, 2)
    z_hi, x_at = tm // 4, lax.rem(tm, 4)

    def local_copy(source, target, sem):
        return pltpu.make_async_copy(source, target, local_sems.at[sem])

    def remote(source, target, sem, device):
        pltpu.make_async_remote_copy(
            src_ref=source, dst_ref=target, send_sem=send_sems.at[sem],
            recv_sem=recv_sems.at[sem], device_id=device, device_id_type=MESH,
        ).start()

    def received(ref, sem):
        pltpu.make_async_copy(ref, ref, recv_sems.at[sem]).wait()

    def sent(ref, sem):
        pltpu.make_async_copy(ref, ref, send_sems.at[sem]).wait()

    loads = [
        local_copy(x_hbm, x_raw, L_X),
        local_copy(wq_s_hbm, wq_s, L_WQS),
        local_copy(wo_s_hbm, wo_s, L_WOS),
        local_copy(cot_hbm.at[pl.ds(2 * tm, 2)], cot_recv.at[:, tm], L_COT),
        local_copy(wq_t_hbm, wq_t, L_WQT),
        local_copy(wo_t_hbm, wo_t, L_WOT),
    ]
    for load in loads:
        load.start()

    barrier = pltpu.get_barrier_semaphore()

    def greet(device):
        pl.semaphore_signal(barrier, inc=1, device_id=device, device_id_type=MESH)

    def greet_station(i, _):
        greet((dp, lax.rem(station + i, 8), tm))
        return 0

    def greet_tm(i, _):
        greet((dp, station, lax.rem(tm + i, 16)))
        return 0

    def greet_dp(i, _):
        greet((1 - dp, station, i * 4 + x_at))
        return 0

    lax.fori_loop(1, 8, greet_station, 0)
    lax.fori_loop(1, 16, greet_tm, 0)
    lax.fori_loop(0, 4, greet_dp, 0)

    loads[0].wait()
    for c in range(4):
        fine[c] = x_raw[:, :, 128 * c : 128 * c + 128].astype(F32).reshape(TOKENS, 128)
    for s in range(8):
        for e in range(2):
            for st in range(2):
                for c in range(4):
                    in_send[s, e, st, :, 128 * c : 128 * c + 128] = fine[
                        c, pl.ds(st * 16 + 2 * s + e, 16, stride=32), :
                    ].astype(BF)
    pl.semaphore_wait(barrier, 26)

    def send_in(i, _):
        p = lax.rem(station + i, 8)
        remote(in_send.at[p], xs.at[:, :, station], R_IN, (dp, p, tm))
        return 0

    lax.fori_loop(1, 8, send_in, 0)

    def send_cot(i, _):
        p = lax.rem(tm + i, 16)
        remote(cot_hbm.at[pl.ds(2 * p, 2)], cot_recv.at[:, tm], R_COT, (dp, station, p))
        return 0

    lax.fori_loop(1, 16, send_cot, 0)
    xs[:, :, station] = in_send[station]

    received(xs.at[:, :, pl.ds(0, 7)], R_IN)
    loads[1].wait()
    loads[2].wait()
    gain_s = gain_s_ref[...]
    _, acted_value = normalise(xs[...].reshape(TOKENS, WIDTH).astype(F32), gain_s)
    acted[0] = acted_value
    joined_s[...] = nn(acted_value, wq_s[...]).astype(BF)

    def forward_loop(step, _):
        forward_step(step, joined_s, probs, att_t.at[0])
        return 0

    lax.fori_loop(0, 2 * PAIRS, forward_loop, 0)
    attended = att_t[0].T
    mid = xs[...].reshape(TOKENS, WIDTH).astype(F32) + nn(attended, wo_s[...])
    pack(lambda k: mid[128 * k : 128 * k + 128], wide, mid_send)

    def send_mid(i, _):
        p = lax.rem(me + i, PEERS)
        remote(mid_send.at[p], mid_recv.at[me], R_MID, (dp, p // 16, lax.rem(p, 16)))
        return 0

    lax.fori_loop(1, PEERS, send_mid, 0)
    mid_recv[me] = mid_send[me]

    loads[3].wait()
    received(cot_recv.at[:, pl.ds(0, 15)], R_COT)
    for c in range(4):
        fine[c] = cot_recv[:, :, :, 128 * c : 128 * c + 128].astype(F32).reshape(TOKENS, 128)
    for st in range(2):
        for e in range(2):
            for s in range(8):
                row = ((st * 2 + e) * 8 + s) * 16
                for c in range(4):
                    ups_t[row : row + 16, 128 * c : 128 * c + 128] = fine[
                        c, pl.ds(st * 256 + 2 * s + e, 16, stride=16), :
                    ].astype(BF)
    loads[4].wait()
    loads[5].wait()
    grad_att[...] = nt(ups_t[...], wo_t[...]).astype(BF)
    acted_t[0] = acted[0].T

    received(mid_recv.at[pl.ds(0, PEERS - 1)], R_MID)

    def put_mid(k, c, value):
        e, st = k // 2, k % 2
        row = (st * 2 + e) * 128
        xt[row : row + 128, 128 * c : 128 * c + 128] = value

    unpack(mid_recv, wide, put_mid)
    gain_t = gain_t_ref[...]
    inverse_t, acted_value = normalise(xt[...], gain_t)
    acted[1] = acted_value
    joined_t[...] = nn(acted_value, wq_t[...]).astype(BF)
    acted_t[1] = acted_value.T

    def time_loop(step, _):
        backward_step(step, joined_t, None, att_t.at[1], grad_att, grad_joined, grad_q_t, True)
        return 0

    lax.fori_loop(0, 2 * PAIRS, time_loop, 0)
    grad_joined[:, 0:WIDTH] = grad_q_t[...].T
    grad_acted = nt(grad_joined[...], wq_t[...])
    gain_sum_t, grad_mid = norm_backward(
        xt[...], inverse_t, gain_t, grad_acted, ups_t[...].astype(F32)
    )

    def grad_mid_block(k):
        e, st = k // 2, k % 2
        row = (st * 2 + e) * 128
        return grad_mid[row : row + 128]

    pack(grad_mid_block, wide, gmid_send)

    def send_gmid(i, _):
        p = lax.rem(me + i, PEERS)
        remote(gmid_send.at[p], gmid_recv.at[me], R_GMID, (dp, p // 16, lax.rem(p, 16)))
        return 0

    lax.fori_loop(1, PEERS, send_gmid, 0)
    gmid_recv[me] = gmid_send[me]

    def sums_begin(layer, base, upstream):
        total[:, :, 0 : 3 * WIDTH] = nn(acted_t[layer], grad_joined[...]).reshape(8, 64, 3 * WIDTH)
        total[:, :, 3 * WIDTH :] = nn(att_t[layer], upstream).reshape(8, 64, WIDTH)

        def fill(i, _):
            pair_send[layer, i] = total[2 * i + 1 - core].astype(BF)
            return 0

        lax.fori_loop(0, 4, fill, 0)
        remote(pair_send.at[layer], pair_recv.at[layer], base, (dp, 2 * y + 1 - core, tm))

    def sums_y(layer, base):
        received(pair_recv.at[layer], base)
        lane = lax.broadcasted_iota(jnp.int32, (1, 128), 1)

        def fill(i, _):
            for j in range(4):
                def part(at):
                    where = pl.ds(at * 128, 128)
                    return total[2 * i + core, :, where] + pair_recv[layer, i, :, where].astype(F32)

                a, b, c, o = part(3 * j), part(3 * j + 1), part(3 * j + 2), part(12 + j)
                turn = lambda v, by: pltpu.roll(v, by, 1)
                y_send[layer, i, 4 * j] = jnp.where(lane < 96, a, turn(o, 96)).astype(BF)
                y_send[layer, i, 4 * j + 1] = jnp.where(
                    lane < 32, turn(a, 32), jnp.where(lane < 96, turn(b, 32), turn(o, 64))
                ).astype(BF)
                y_send[layer, i, 4 * j + 2] = jnp.where(
                    lane < 64, turn(b, 64), jnp.where(lane < 96, turn(c, 64), turn(o, 32))
                ).astype(BF)
                y_send[layer, i, 4 * j + 3] = jnp.where(lane < 96, turn(c, 96), o).astype(BF)
            return 0

        lax.fori_loop(0, 4, fill, 0)

        def send(i, _):
            p = lax.rem(y + i, 4)
            remote(y_send.at[layer, p], y_recv.at[layer, y], base + 1, (dp, 2 * p + core, tm))
            return 0

        lax.fori_loop(1, 4, send, 0)
        y_recv[layer, y] = y_send[layer, y]

    def sums_x(layer, base):
        received(y_recv.at[layer, pl.ds(0, 3)], base + 1)

        def add(i, _):
            value = y_recv[layer, 0, i].astype(F32)
            for j in range(1, 4):
                value = value + y_recv[layer, j, i].astype(F32)
            x_send[layer, lax.rem(i, 4), i // 4] = value.astype(BF)
            return 0

        lax.fori_loop(0, 16, add, 0)

        def send(i, _):
            p = lax.rem(x_at + i, 4)
            remote(x_send.at[layer, p], x_recv.at[layer, x_at], base + 2, (dp, station, z_hi * 4 + p))
            return 0

        lax.fori_loop(1, 4, send, 0)
        x_recv[layer, x_at] = x_send[layer, x_at]

    def sums_z(layer, base):
        received(x_recv.at[layer, pl.ds(0, 3)], base + 2)
        value = x_recv[layer, 0].astype(F32)
        for j in range(1, 4):
            value = value + x_recv[layer, j].astype(F32)
        z_send[layer] = value.astype(BF)
        mine = 2 * z_hi + dp

        def send(i, _):
            p = lax.rem(mine + i, 8)
            remote(
                z_send.at[layer, p // 2], z_recv.at[layer, mine], base + 3,
                (lax.rem(p, 2), station, (p // 2) * 4 + x_at),
            )
            return 0

        lax.fori_loop(1, 8, send, 0)
        z_recv[layer, mine] = z_send[layer, z_hi]

    def sums_end(layer, base, qkv_ref, out_ref):
        received(z_recv.at[layer, pl.ds(0, 7)], base + 3)
        value = z_recv[layer, 0].astype(F32)
        for j in range(1, 8):
            value = value + z_recv[layer, j].astype(F32)
        qkv_ref[...] = value[:, 0:96].astype(BF)
        out_ref[...] = pltpu.roll(value, 32, 1)[:, 0:32].astype(BF)

    sums_begin(1, R_TIME, ups_t[...])
    sums_y(1, R_TIME)

    received(gmid_recv.at[pl.ds(0, PEERS - 1)], R_GMID)

    def put_gmid(k, c, value):
        ups_s[128 * k : 128 * k + 128, 128 * c : 128 * c + 128] = value.astype(BF)

    unpack(gmid_recv, wide, put_gmid)
    grad_att[...] = nt(ups_s[...], wo_s[...]).astype(BF)

    def station_loop(step, _):
        backward_step(step, joined_s, probs, att_t.at[0], grad_att, grad_joined, grad_q_t, False)
        return 0

    lax.fori_loop(0, 2 * PAIRS, station_loop, 0, unroll=8)
    grad_joined[:, 0:WIDTH] = grad_q_t[...].T
    sums_x(1, R_TIME)
    grad_acted = nt(grad_joined[...], wq_s[...])
    x_value = xs[...].reshape(TOKENS, WIDTH).astype(F32)
    inverse_s = lax.rsqrt(jnp.mean(x_value * x_value, axis=1, keepdims=True) + EPSILON)
    gain_sum_s, grad_in = norm_backward(
        x_value, inverse_s, gain_s, grad_acted, ups_s[...].astype(F32)
    )
    gin_send[...] = grad_in.astype(BF).reshape(2, 2, 8, 16, WIDTH)

    def send_gin(i, _):
        p = lax.rem(station + i, 8)
        remote(gin_send.at[:, :, p], gin_recv.at[station], R_GIN, (dp, p, tm))
        return 0

    lax.fori_loop(1, 8, send_gin, 0)
    gin_recv[station] = gin_send[:, :, station]

    for c in range(4):
        gain_send[0, c : c + 1, :] = gain_sum_s[:, 128 * c : 128 * c + 128]
        gain_send[0, 4 + c : 5 + c, :] = gain_sum_t[:, 128 * c : 128 * c + 128]

    def send_gain_s(i, _):
        p = lax.rem(station + i, 8)
        remote(gain_send.at[0], gain_s_recv.at[station], R_GAIN_S, (dp, p, tm))
        return 0

    lax.fori_loop(1, 8, send_gain_s, 0)
    gain_s_recv[station] = gain_send[0]

    sums_begin(0, R_STATION, ups_s[...])
    sums_z(1, R_TIME)
    sums_y(0, R_STATION)

    received(gain_s_recv.at[pl.ds(0, 7)], R_GAIN_S)
    value = gain_s_recv[0]
    for j in range(1, 8):
        value = value + gain_s_recv[j]
    gain_send[1] = value

    def send_gain_x(i, _):
        p = lax.rem(x_at + i, 4)
        remote(gain_send.at[1], gain_x_recv.at[x_at], R_GAIN_X, (dp, station, z_hi * 4 + p))
        return 0

    lax.fori_loop(1, 4, send_gain_x, 0)
    gain_x_recv[x_at] = value

    sums_end(1, R_TIME, gq_t_ref, go_t_ref)

    received(gin_recv.at[pl.ds(0, 7)], R_GIN)
    for s in range(8):
        for e in range(2):
            for st in range(2):
                for c in range(4):
                    fine[c, pl.ds(st * 16 + 2 * s + e, 16, stride=32), :] = gin_recv[
                        s, e, st, :, 128 * c : 128 * c + 128
                    ].astype(F32)
    for c in range(4):
        gin_ref[:, :, 128 * c : 128 * c + 128] = fine[c].astype(BF).reshape(32, 16, 128)

    received(gain_x_recv.at[pl.ds(0, 3)], R_GAIN_X)
    value = gain_x_recv[0]
    for j in range(1, 4):
        value = value + gain_x_recv[j]
    gain_send[2] = value
    mine = 2 * z_hi + dp

    def send_gain_z(i, _):
        p = lax.rem(mine + i, 8)
        remote(
            gain_send.at[2], gain_z_recv.at[mine], R_GAIN_Z,
            (lax.rem(p, 2), station, (p // 2) * 4 + x_at),
        )
        return 0

    lax.fori_loop(1, 8, send_gain_z, 0)
    gain_z_recv[mine] = value

    sums_x(0, R_STATION)
    received(gain_z_recv.at[pl.ds(0, 7)], R_GAIN_Z)
    value = gain_z_recv[0]
    for j in range(1, 8):
        value = value + gain_z_recv[j]
    for c in range(4):
        gg_s_ref[:, 128 * c : 128 * c + 128] = value[c : c + 1]
        gg_t_ref[:, 128 * c : 128 * c + 128] = value[4 + c : 5 + c]
    sums_z(0, R_STATION)
    sums_end(0, R_STATION, gq_s_ref, go_s_ref)

    sent(in_send.at[pl.ds(0, 7)], R_IN)
    sent(cot_recv.at[:, pl.ds(0, 15)], R_COT)
    sent(mid_send.at[pl.ds(0, PEERS - 1)], R_MID)
    sent(gmid_send.at[pl.ds(0, PEERS - 1)], R_GMID)
    sent(gin_recv.at[pl.ds(0, 7)], R_GIN)
    sent(gain_s_recv.at[pl.ds(0, 7)], R_GAIN_S)
    sent(gain_x_recv.at[pl.ds(0, 3)], R_GAIN_X)
    sent(gain_z_recv.at[pl.ds(0, 7)], R_GAIN_Z)
    for layer, base in ((1, R_TIME), (0, R_STATION)):
        sent(pair_send.at[layer], base)
        sent(y_recv.at[layer, pl.ds(0, 3)], base + 1)
        sent(x_recv.at[layer, pl.ds(0, 3)], base + 2)
        sent(z_recv.at[layer, pl.ds(0, 7)], base + 3)


def local(inputs, cotangent, station_gain, station_qkv, station_out, time_gain, time_qkv, time_out):
    any_space = pl.BlockSpec(memory_space=pl.ANY)
    vmem = pl.BlockSpec(memory_space=pltpu.VMEM)
    shape = jax.ShapeDtypeStruct
    results = pl.pallas_call(
        kernel,
        out_shape=(
            shape((32, 16, WIDTH), BF),
            shape((64, 96), BF), shape((64, 32), BF), shape((1, WIDTH), F32),
            shape((64, 96), BF), shape((64, 32), BF), shape((1, WIDTH), F32),
        ),
        in_specs=[any_space, any_space, vmem, any_space, any_space, vmem, any_space, any_space],
        out_specs=[vmem] * 7,
        scratch_shapes=[
            pltpu.VMEM((32, 16, WIDTH), BF),
            pltpu.VMEM((4, TOKENS, 128), F32),
            pltpu.VMEM((PEERS * 16, 128), F32),
            pltpu.VMEM((8, 2, 2, 16, WIDTH), BF),
            pltpu.VMEM((2, 2, 8, 16, WIDTH), BF),
            pltpu.VMEM((2, 16, 16, WIDTH), BF),
            pltpu.VMEM((TOKENS, WIDTH), BF),
            pltpu.VMEM((WIDTH, 3 * WIDTH), BF),
            pltpu.VMEM((WIDTH, WIDTH), BF),
            pltpu.VMEM((WIDTH, 3 * WIDTH), BF),
            pltpu.VMEM((WIDTH, WIDTH), BF),
            pltpu.VMEM((2, TOKENS, WIDTH), BF),
            pltpu.VMEM((TOKENS, 3 * WIDTH), BF),
            pltpu.VMEM((TOKENS, 3 * WIDTH), BF),
            pltpu.VMEM((16, SEQ, SEQ), F32),
            pltpu.VMEM((2, WIDTH, TOKENS), BF),
            pltpu.VMEM((TOKENS, WIDTH), BF),
            pltpu.VMEM((TOKENS, 3 * WIDTH), BF),
            pltpu.VMEM((WIDTH, TOKENS), BF),
            pltpu.VMEM((2, WIDTH, TOKENS), BF),
            pltpu.VMEM((PEERS, 16, 128), BF),
            pltpu.VMEM((PEERS, 16, 128), BF),
            pltpu.VMEM((TOKENS, WIDTH), F32),
            pltpu.VMEM((PEERS, 16, 128), BF),
            pltpu.VMEM((PEERS, 16, 128), BF),
            pltpu.VMEM((TOKENS, WIDTH), BF),
            pltpu.VMEM((2, 2, 8, 16, WIDTH), BF),
            pltpu.VMEM((8, 2, 2, 16, WIDTH), BF),
            pltpu.VMEM((8, 64, 4 * WIDTH), F32),
            pltpu.VMEM((2, 4, 64, 4 * WIDTH), BF),
            pltpu.VMEM((2, 4, 64, 4 * WIDTH), BF),
            pltpu.VMEM((2, 4, 16, 64, 128), BF),
            pltpu.VMEM((2, 4, 16, 64, 128), BF),
            pltpu.VMEM((2, 4, 4, 64, 128), BF),
            pltpu.VMEM((2, 4, 4, 64, 128), BF),
            pltpu.VMEM((2, 4, 64, 128), BF),
            pltpu.VMEM((2, 8, 64, 128), BF),
            pltpu.VMEM((3, 8, 128), F32),
            pltpu.VMEM((8, 8, 128), F32),
            pltpu.VMEM((4, 8, 128), F32),
            pltpu.VMEM((8, 8, 128), F32),
            pltpu.SemaphoreType.DMA((N_SEMS,)),
            pltpu.SemaphoreType.DMA((N_SEMS,)),
            pltpu.SemaphoreType.DMA((6,)),
        ],
        compiler_params=pltpu.CompilerParams(
            collective_id=0, has_side_effects=True, vmem_limit_bytes=60 * 2**20
        ),
    )(
        inputs.reshape(32, 16, WIDTH), cotangent.reshape(32, 16, WIDTH),
        station_gain.reshape(1, WIDTH), station_qkv, station_out,
        time_gain.reshape(1, WIDTH), time_qkv, time_out,
    )
    grad_in, qkv_s, out_s, gain_s, qkv_t, out_t, gain_t = results
    return (
        grad_in.reshape(inputs.shape),
        qkv_s, out_s, gain_s.reshape(WIDTH), qkv_t, out_t, gain_t.reshape(WIDTH),
    )


def solution(mesh):
    rows = P("dp", "station", "tm", None)
    split = P("station", "tm")
    return jax.shard_map(
        local,
        mesh=mesh,
        in_specs=(rows, rows, P(), P(), P(), P(), P(), P()),
        out_specs=(rows, split, split, P(), split, split, P()),
        check_vma=False,
    )
```

time: 702 us -> 124 us (0.18); the launches traced: 691 us -> 122 us
  waiting for transfers between devices: 345 us -> 0 us
  blocking collectives: 127 us -> 0 us
  Pallas kernels: 0 us -> 112 us
  local copies, waits for them, and re-layouts: 93.1 us -> 9.79 us
  matrix products: 77.2 us -> 0 us
  starting transfers between devices: 29.9 us -> 0 us
  between operations: 14.9 us -> 0.65 us
    reduce_scatter x4 -> x0, waiting for transfers between devices: 260 us -> none  [the longest x2 173 us: reduce_weights(): lax.psum_scatter(first_grad.astype(jnp.bfloat16), 'tm', scatter_dimension...]
    pallas_call x0 -> x1, Pallas kernels: none -> 112 us  [local(): pl.pallas_call(kernel, out_shape=(shape((32, 16, WIDTH), BF), shape((64,...]
    psum x2 -> x0, blocking collectives: 83.6 us -> none  [the longest x1 74.1 us: local(): lax.psum((station_gain_part, time_gain_part), ('dp', 'station', 'tm'))]
    dot_general x23 -> x0, matrix products: 77.2 us -> none  [the longest x2 17.9 us: backward_from(): jnp.einsum('achlm,alche->amche', grad_scores, queries, preferred_element_...]
    unnamed x12 -> x0, waiting for transfers between devices: 57.1 us -> none
    all_to_all x3 -> x0, blocking collectives: 43.1 us -> none  [the longest x1 14.7 us: local(): lax.all_to_all(inputs, 'station', split_axis=2, concat_axis=1, tiled=True)]
    another operation x17 -> x0, local copies, waits for them, and re-layouts: 37.1 us -> none
    all_to_all x4 -> x0, starting transfers between devices: 29.2 us -> none  [the longest x1 11.4 us: local(): lax.all_to_all(cotangent, 'tm', split_axis=1, concat_axis=2, tiled=True)]
  transfers between devices with their start and end apart: 12 -> 0, of which waited for: 9 -> 0; matrix products, arithmetic and copies ran while one was open for 12% -> 0% of each run, Pallas kernels for 0% -> 0%
where the time goes in v1:
time: 124 us; the launch traced here: 122 us
  Pallas kernels  112 us (90%)
  local copies, waits for them, and re-layouts  9.79 us (8%)
    pallas_call x1, Pallas kernels, local(): pl.pallas_call(kernel, out_shape=(shape((32, 16, WIDTH), BF), shape((64,...  112 us
    unnamed x7, local copies, waits for them, and re-layouts  9.79 us

profile of v1, /device:TPU:6, one launch (start us, length us, event | category | flops | bytes accessed | tf_op | source)
XLA Modules:
  0.0 122.4 jit_solution(7419381493735656716)
XLA Ops:
  0.6 111.9 %shard_map.135 = (bf16[32,16,512]{2,1,0:T(8,128)(2,1)}, bf16[64,96]{1,0:T(8,128)(2,1)}, bf16[64,32]{1,0:T(8,128)(2,1)}, f32[1,512]{1,0:T(1,128)}, bf16[64,96]{1,...) custom-call(bf16[32,16,512]{2,1,0:T(8,128)(2,1)} %bitcast.7, bf16[32,16,512]{2,1,0:T(8,128)(2,1)} %bitcast.8, ...), custom_call_target="tpu_custom_call" | custom-call | tf_op jit(solution)/shard_map/pallas_call | solution.py:521
  112.6 1.4 %copy.15 = bf16[64,32]{0,1:T(8,128)(2,1)} copy(bf16[64,32]{1,0:T(8,128)(2,1)} %get-tuple-element.23) | data formatting | bytes 8192
  114.0 1.4 %copy.16 = bf16[64,32]{0,1:T(8,128)(2,1)} copy(bf16[64,32]{1,0:T(8,128)(2,1)} %get-tuple-element.26) | data formatting | bytes 8192
  115.4 1.9 %copy.22 = bf16[1,32,16,512]{3,2,1,0:T(8,128)(2,1)} copy(bf16[1,32,16,512]{3,2,1,0:T(8,128)(2,1)} %bitcast.9) | data formatting | bytes 1048576
  117.2 1.3 %copy.23 = bf16[64,96]{1,0:T(8,128)(2,1)} copy(bf16[64,96]{1,0:T(8,128)(2,1)} %get-tuple-element.36) | data formatting | bytes 24576
  118.6 1.3 %copy.24 = f32[512]{0:T(512)} copy(f32[512]{0:T(512)} %bitcast.13) | data formatting | bytes 4096
  119.8 1.3 %copy.25 = bf16[64,96]{1,0:T(8,128)(2,1)} copy(bf16[64,96]{1,0:T(8,128)(2,1)} %get-tuple-element.39) | data formatting | bytes 24576
  121.1 1.2 %copy.26 = f32[512]{0:T(512)} copy(f32[512]{0:T(512)} %bitcast.12) | data formatting | bytes 4096

commit v2 on v1

v2 whole, which is shorter than its diff:
```python
import functools

import jax
import jax.numpy as jnp
from jax import lax
from jax.experimental import pallas as pl
from jax.experimental.pallas import tpu as pltpu
from jax.sharding import PartitionSpec as P

MESH = pl.DeviceIdType.MESH
BF = jnp.bfloat16
F32 = jnp.float32
EPSILON = 1e-05
WIDTH = 512
TOKENS = 512
SEQ = 256
PAIRS = 4
PEERS = 128

R_IN, R_COT, R_GIN, R_GAIN_S, R_GAIN_X, R_GAIN_Z, R_MID, R_GMID, R_TIME, R_STATION = (
    0, 1, 2, 3, 4, 5, 6, 8, 10, 16,
)
PAIR, FIRST_Y, FIRST_X, SECOND_X, SECOND_Y, THIRD = range(6)
N_SEMS = 22
L_X, L_COT, L_WQS, L_WOS, L_WQT, L_WOT = range(6)
CHUNK = 128


def nn(a, b):
    return jnp.dot(a, b, preferred_element_type=F32)


def nt(a, b):
    return lax.dot_general(a, b, (((1,), (1,)), ((), ())), preferred_element_type=F32)


def tn(a, b):
    return lax.dot_general(a, b, (((0,), (0,)), ((), ())), preferred_element_type=F32)


def columns(pair, base=0):
    return slice(base + pair * 128, base + pair * 128 + 128)


def half_masks(value):
    lane = lax.broadcasted_iota(jnp.int32, (1, 128), 1)
    first = jnp.where(lane < 64, value, 0.0).astype(BF)
    second = jnp.where(lane < 64, 0.0, value).astype(BF)
    return first, second


def stacked(block, masks):
    return jnp.concatenate([block * masks[0], block * masks[1]], axis=0)


def under(block):
    return jnp.concatenate([block[:, :CHUNK], block[:, CHUNK:]], axis=0)


def softmax_t(scores):
    expon = jnp.exp(scores)
    total = jnp.sum(expon, axis=0, keepdims=True)
    shrink = jnp.where(total > 1.0, 0.25, 1.0)
    return (expon * shrink) * (1.0 / (total * shrink))


def forward_part(seq, pair, part, joined, probs, attended):
    rows = slice(seq * SEQ, seq * SEQ + SEQ)
    own = slice(seq * SEQ + part * CHUNK, seq * SEQ + part * CHUNK + CHUNK)
    queries = stacked(joined[own, columns(pair)], half_masks(0.125))
    values = stacked(joined[rows, columns(pair, 2 * WIDTH)], half_masks(1.0))
    p = softmax_t(nt(joined[rows, columns(pair, WIDTH)], queries))
    probs[seq * PAIRS + pair, :, part * 2 * CHUNK : part * 2 * CHUNK + 2 * CHUNK] = p
    attended[own, columns(pair)] = tn(under(p.astype(BF)), values).astype(BF)


def backward_step(seq, pair, joined, probs, attended, grad_att, grad_joined):
    rows = slice(seq * SEQ, seq * SEQ + SEQ)
    eighths = half_masks(0.125)
    ones = half_masks(1.0)
    keys = joined[rows, columns(pair, WIDTH)]
    values = joined[rows, columns(pair, 2 * WIDTH)]
    key_rows = stacked(keys, eighths)
    if probs is None:
        value_rows = stacked(values, ones)
    qs, us, p_halves, grad_ss = [], [], [], []
    for part in range(SEQ // CHUNK):
        own = slice(seq * SEQ + part * CHUNK, seq * SEQ + part * CHUNK + CHUNK)
        q = stacked(joined[own, columns(pair)], eighths)
        u = stacked(grad_att[own, columns(pair)], ones)
        if probs is None:
            p = softmax_t(nt(keys, q))
        else:
            p = probs[seq * PAIRS + pair, :, part * 2 * CHUNK : part * 2 * CHUNK + 2 * CHUNK]
        p_half = p.astype(BF)
        if probs is None:
            attended[own, columns(pair)] = tn(under(p_half), value_rows).astype(BF)
        grad_p = nt(values, u)
        dot = jnp.sum(grad_p * p, axis=0, keepdims=True)
        grad_s = (p * (grad_p - dot)).astype(BF)
        grad_joined[own, columns(pair)] = tn(under(grad_s), key_rows).astype(BF)
        qs.append(q)
        us.append(u)
        p_halves.append(p_half)
        grad_ss.append(grad_s)
    join = jnp.concatenate
    grad_joined[rows, columns(pair, WIDTH)] = nn(join(grad_ss, axis=1), join(qs, axis=0)).astype(BF)
    grad_joined[rows, columns(pair, 2 * WIDTH)] = nn(
        join(p_halves, axis=1), join(us, axis=0)
    ).astype(BF)


def normalise(x, gain):
    inverse = lax.rsqrt(jnp.mean(x * x, axis=1, keepdims=True) + EPSILON)
    normed = x * inverse
    return inverse, (normed * gain).astype(BF)


def norm_backward(x, inverse, gain, grad_acted, upstream):
    normed = x * inverse
    grad_gain = jnp.sum(grad_acted * normed, axis=0, keepdims=True)
    grad_normed = grad_acted * gain
    mean = jnp.mean(grad_normed * normed, axis=1, keepdims=True)
    return grad_gain, upstream + inverse * (grad_normed - normed * mean)


def part_rows(ref, part):
    return jnp.concatenate([ref[part * 128 : part * 128 + 128], ref[256 + part * 128 : 384 + part * 128]], axis=0)


def put_rows(ref, part, value):
    ref[part * 128 : part * 128 + 128] = value[0:128]
    ref[256 + part * 128 : 384 + part * 128] = value[128:256]


def place(a, b, epoch_first):
    return a * 2 + b if epoch_first else b * 2 + a


def pack(value, part, epoch_first, wide, send):
    for a in range(2):
        for b in range(2):
            block = value[a * 128 + b * 64 : a * 128 + b * 64 + 64]
            for c in range(4):
                wide[
                    pl.ds(part * 1024 + c * 4 + place(a, b, epoch_first), 64, stride=16), :
                ] = block[:, 128 * c : 128 * c + 128]
    send[part] = wide[part * 1024 : part * 1024 + 1024].astype(BF).reshape(64, 16, 128)


def unpack(recv, part, epoch_first, wide, target):
    wide[part * 1024 : part * 1024 + 1024] = recv[part].reshape(1024, 128).astype(F32)
    for a in range(2):
        for b in range(2):
            row = a * 256 + part * 128 + b * 64
            for c in range(4):
                target[row : row + 64, 128 * c : 128 * c + 128] = wide[
                    pl.ds(part * 1024 + c * 4 + place(a, b, epoch_first), 64, stride=16), :
                ].astype(target.dtype)


def kernel(
    x_hbm, cot_hbm, gain_s_ref, wq_s_hbm, wo_s_hbm, gain_t_ref, wq_t_hbm, wo_t_hbm,
    gin_ref, sums_ref, gains_ref,
    x_raw, fine, wide, in_send, xs, cot_recv, ups_t, wq_s, wo_s, wq_t, wo_t,
    acted, joined_s, joined_t, probs, attended, grad_att, grad_joined, acted_t, att_t,
    mid_send, mid_recv, xt, gmid_send, gmid_recv, ups_s, gin_send, gin_recv,
    total, pair_send, pair_recv, y_send, y_recv, x1_send, x1_recv,
    xb_send, xb_recv, yb_send, yb_recv, z_send, z_recv,
    gain_send, gain_s_recv, gain_x_recv, gain_z_recv,
    send_sems, recv_sems, local_sems,
):
    dp, station, tm = lax.axis_index("dp"), lax.axis_index("station"), lax.axis_index("tm")
    y, core = station // 2, lax.rem(station, 2)
    z_hi, x_at = tm // 4, lax.rem(tm, 4)
    spot = y * 16 + tm

    def local_copy(source, target, sem):
        return pltpu.make_async_copy(source, target, local_sems.at[sem])

    def remote(source, target, sem, device):
        pltpu.make_async_remote_copy(
            src_ref=source, dst_ref=target, send_sem=send_sems.at[sem],
            recv_sem=recv_sems.at[sem], device_id=device, device_id_type=MESH,
        ).start()

    def received(ref, sem):
        pltpu.make_async_copy(ref, ref, recv_sems.at[sem]).wait()

    def sent(ref, sem):
        pltpu.make_async_copy(ref, ref, send_sems.at[sem]).wait()

    def each(first, last, action):
        def step(i, _):
            action(i)
            return 0

        lax.fori_loop(first, last, step, 0)

    loads = [
        local_copy(x_hbm, x_raw, L_X),
        local_copy(wq_s_hbm, wq_s, L_WQS),
        local_copy(wo_s_hbm, wo_s, L_WOS),
        local_copy(cot_hbm.at[pl.ds(2 * tm, 2)], cot_recv.at[:, tm], L_COT),
        local_copy(wq_t_hbm, wq_t, L_WQT),
        local_copy(wo_t_hbm, wo_t, L_WOT),
    ]
    for load in loads:
        load.start()

    barrier = pltpu.get_barrier_semaphore()

    def greet(device):
        pl.semaphore_signal(barrier, inc=1, device_id=device, device_id_type=MESH)

    each(1, 8, lambda i: greet((dp, lax.rem(station + i, 8), tm)))
    each(1, 16, lambda i: greet((dp, station, lax.rem(tm + i, 16))))
    each(0, 4, lambda i: greet((1 - dp, station, i * 4 + x_at)))

    loads[0].wait()
    for c in range(4):
        fine[c] = x_raw[:, :, 128 * c : 128 * c + 128].astype(F32).reshape(TOKENS, 128)
    for s in range(8):
        for e in range(2):
            for st in range(2):
                for c in range(4):
                    in_send[s, e, st, :, 128 * c : 128 * c + 128] = fine[
                        c, pl.ds(st * 16 + 2 * s + e, 16, stride=32), :
                    ].astype(BF)
    pl.semaphore_wait(barrier, 26)

    def send_in(i):
        p = lax.rem(station + i, 8)
        remote(
            in_send.at[p], xs.at[:, lax.rem(station + p, 2), :, y], R_IN, (dp, p, tm)
        )

    def send_cot(i):
        p = lax.rem(tm + i, 16)
        remote(cot_hbm.at[pl.ds(2 * p, 2)], cot_recv.at[:, tm], R_COT, (dp, station, p))

    each(1, 8, send_in)
    each(1, 16, send_cot)
    xs[:, 0, :, y] = in_send[station]

    received(in_send.at[pl.ds(0, 7)], R_IN)
    loads[1].wait()
    gain_s = gain_s_ref[...]
    _, acted_value = normalise(xs[...].reshape(TOKENS, WIDTH).astype(F32), gain_s)
    acted[0] = acted_value
    joined_s[...] = nn(acted_value, wq_s[...]).astype(BF)
    loads[2].wait()

    def send_parts(send, recv, sem, part):
        other = lax.rem(core + part, 2)

        def action(i):
            p = lax.rem(spot + i, 64)
            remote(
                send.at[part, p], recv.at[part, spot], sem + part,
                (dp, 2 * (p // 16) + other, lax.rem(p, 16)),
            )

        each(1 - part, 64, action)

    for part in range(2):
        for seq in range(2):
            for pair in range(PAIRS):
                forward_part(seq, pair, part, joined_s, probs, attended.at[0])
        x_part = jnp.concatenate(
            [xs[0, part].reshape(128, WIDTH), xs[1, part].reshape(128, WIDTH)], axis=0
        )
        mid = x_part.astype(F32) + nn(part_rows(attended.at[0], part), wo_s[...])
        pack(mid, part, True, wide, mid_send)
        send_parts(mid_send, mid_recv, R_MID, part)
    mid_recv[0, spot] = mid_send[0, spot]

    loads[3].wait()
    received(cot_recv.at[:, pl.ds(0, 15)], R_COT)
    for c in range(4):
        fine[c] = cot_recv[:, :, :, 128 * c : 128 * c + 128].astype(F32).reshape(TOKENS, 128)
    for s in range(8):
        part = lax.rem(core + s, 2)
        for st in range(2):
            for e in range(2):
                for c in range(4):
                    ups_t[st, part, e, s // 2, :, 128 * c : 128 * c + 128] = fine[
                        c, pl.ds(st * 256 + 2 * s + e, 16, stride=16), :
                    ].astype(BF)
    loads[4].wait()
    loads[5].wait()
    upstream_t = ups_t[...].reshape(TOKENS, WIDTH)
    grad_att[...] = nt(upstream_t, wo_t[...]).astype(BF)
    acted_t[0] = acted[0].T.reshape(4, 2, 64, TOKENS)
    att_t[0] = attended[0].T.reshape(4, 2, 64, TOKENS)

    gain_t = gain_t_ref[...]
    for part in range(2):
        received(mid_recv.at[part, pl.ds(0, 63 + part)], R_MID + part)
        unpack(mid_recv, part, False, wide, xt)
        _, acted_value = normalise(part_rows(xt, part), gain_t)
        put_rows(acted.at[1], part, acted_value)
        put_rows(joined_t, part, nn(acted_value, wq_t[...]).astype(BF))

    for seq in range(2):
        for pair in range(PAIRS):
            backward_step(seq, pair, joined_t, None, attended.at[1], grad_att, grad_joined)
    gain_sum_t = None
    for part in range(2):
        x_value = part_rows(xt, part)
        inverse = lax.rsqrt(jnp.mean(x_value * x_value, axis=1, keepdims=True) + EPSILON)
        grad_acted = nt(part_rows(grad_joined, part), wq_t[...])
        up_part = jnp.concatenate(
            [ups_t[0, part].reshape(128, WIDTH), ups_t[1, part].reshape(128, WIDTH)], axis=0
        )
        gain_part, grad_mid = norm_backward(
            x_value, inverse, gain_t, grad_acted, up_part.astype(F32)
        )
        gain_sum_t = gain_part if gain_sum_t is None else gain_sum_t + gain_part
        pack(grad_mid, part, False, wide, gmid_send)
        send_parts(gmid_send, gmid_recv, R_GMID, part)
    gmid_recv[0, spot] = gmid_send[0, spot]

    def products(layer, who, upstream):
        left = acted_t[layer, :, who].reshape(256, TOKENS)
        left_out = att_t[layer, :, who].reshape(256, TOKENS)
        return (
            nn(left, grad_joined[...]).reshape(4, 64, 3 * WIDTH),
            nn(left_out, upstream).reshape(4, 64, WIDTH),
        )

    def sums_send(layer, base, upstream):
        qkv, out = products(layer, 1 - core, upstream)
        pair_send[layer, :, :, 0 : 3 * WIDTH] = qkv.astype(BF)
        pair_send[layer, :, :, 3 * WIDTH :] = out.astype(BF)
        remote(pair_send.at[layer], pair_recv.at[layer], base + PAIR, (dp, 2 * y + 1 - core, tm))

    def sums_own(layer, upstream):
        qkv, out = products(layer, core, upstream)
        total[:, :, 0 : 3 * WIDTH] = qkv
        total[:, :, 3 * WIDTH :] = out

    def sums_first(layer, base):
        received(pair_recv.at[layer], base + PAIR)
        lane = lax.broadcasted_iota(jnp.int32, (1, 128), 1)

        def fill(i):
            def put(t, value):
                value = value.astype(BF)
                y_send[layer, i, t] = value[0:32]
                x1_send[layer, t % 4, i, t // 4] = value[32:64]

            for j in range(4):
                def piece(at):
                    where = slice(at * 128, at * 128 + 128)
                    return total[i, :, where] + pair_recv[layer, i, :, where].astype(F32)

                a, b, c, o = piece(3 * j), piece(3 * j + 1), piece(3 * j + 2), piece(12 + j)
                turn = lambda v, by: pltpu.roll(v, by, 1)
                put(4 * j, jnp.where(lane < 96, a, turn(o, 96)))
                put(4 * j + 1, jnp.where(lane < 32, turn(a, 32), jnp.where(lane < 96, turn(b, 32), turn(o, 64))))
                put(4 * j + 2, jnp.where(lane < 64, turn(b, 64), jnp.where(lane < 96, turn(c, 64), turn(o, 32))))
                put(4 * j + 3, jnp.where(lane < 96, turn(c, 96), o))

        each(0, 4, fill)

        def send_x(i):
            p = lax.rem(x_at + i, 4)
            remote(
                x1_send.at[layer, p], x1_recv.at[layer, x_at], base + FIRST_X,
                (dp, station, z_hi * 4 + p),
            )

        def send_y(i):
            p = lax.rem(y + i, 4)
            remote(
                y_send.at[layer, p], y_recv.at[layer, y], base + FIRST_Y, (dp, 2 * p + core, tm)
            )

        each(1, 4, send_x)
        each(1, 4, send_y)
        y_recv[layer, y] = y_send[layer, y]
        x1_recv[layer, x_at] = x1_send[layer, x_at]

    def sums_second(layer, base):
        received(x1_recv.at[layer, pl.ds(0, 3)], base + FIRST_X)

        def add_x(i):
            value = x1_recv[layer, 0, i].astype(F32)
            for j in range(1, 4):
                value = value + x1_recv[layer, j, i].astype(F32)
            yb_send[layer, i] = value.astype(BF)

        each(0, 4, add_x)

        def send_y(i):
            p = lax.rem(y + i, 4)
            remote(
                yb_send.at[layer, p], yb_recv.at[layer, y], base + SECOND_Y, (dp, 2 * p + core, tm)
            )

        each(1, 4, send_y)
        yb_recv[layer, y] = yb_send[layer, y]

        received(y_recv.at[layer, pl.ds(0, 3)], base + FIRST_Y)

        def add_y(i):
            for at in range(4):
                value = y_recv[layer, 0, 4 * i + at].astype(F32)
                for j in range(1, 4):
                    value = value + y_recv[layer, j, 4 * i + at].astype(F32)
                xb_send[layer, at, i] = value.astype(BF)

        each(0, 4, add_y)

        def send_x(i):
            p = lax.rem(x_at + i, 4)
            remote(
                xb_send.at[layer, p], xb_recv.at[layer, x_at], base + SECOND_X,
                (dp, station, z_hi * 4 + p),
            )

        each(1, 4, send_x)
        xb_recv[layer, x_at] = xb_send[layer, x_at]

    def sums_third(layer, base):
        received(yb_recv.at[layer, pl.ds(0, 3)], base + SECOND_Y)
        received(xb_recv.at[layer, pl.ds(0, 3)], base + SECOND_X)
        low, high = xb_recv[layer, 0].astype(F32), yb_recv[layer, 0].astype(F32)
        for j in range(1, 4):
            low = low + xb_recv[layer, j].astype(F32)
            high = high + yb_recv[layer, j].astype(F32)
        z_send[layer, :, 0:32] = low.astype(BF)
        z_send[layer, :, 32:64] = high.astype(BF)
        mine = 2 * z_hi + dp

        def send(i):
            p = lax.rem(mine + i, 8)
            remote(
                z_send.at[layer, p // 2], z_recv.at[layer, mine], base + THIRD,
                (lax.rem(p, 2), station, (p // 2) * 4 + x_at),
            )

        each(1, 8, send)
        z_recv[layer, mine] = z_send[layer, z_hi]

    def sums_end(layer, base):
        received(z_recv.at[layer, pl.ds(0, 7)], base + THIRD)
        value = z_recv[layer, 0].astype(F32)
        for j in range(1, 8):
            value = value + z_recv[layer, j].astype(F32)
        sums_ref[layer] = value.astype(BF)

    acted_t[1] = acted[1].T.reshape(4, 2, 64, TOKENS)
    att_t[1] = attended[1].T.reshape(4, 2, 64, TOKENS)
    sums_send(1, R_TIME, upstream_t)
    sums_own(1, upstream_t)
    sums_first(1, R_TIME)

    for part in range(2):
        received(gmid_recv.at[part, pl.ds(0, 63 + part)], R_GMID + part)
        unpack(gmid_recv, part, True, wide, ups_s)
        put_rows(grad_att, part, nt(part_rows(ups_s, part), wo_s[...]).astype(BF))
    for seq in range(2):
        for pair in range(PAIRS):
            backward_step(seq, pair, joined_s, probs, None, grad_att, grad_joined)
    sums_send(0, R_STATION, ups_s[...])
    sums_second(1, R_TIME)
    grad_acted = nt(grad_joined[...], wq_s[...])
    x_value = xs[...].reshape(TOKENS, WIDTH).astype(F32)
    inverse_s = lax.rsqrt(jnp.mean(x_value * x_value, axis=1, keepdims=True) + EPSILON)
    gain_sum_s, grad_in = norm_backward(
        x_value, inverse_s, gain_s, grad_acted, ups_s[...].astype(F32)
    )
    gin_send[...] = grad_in.astype(BF).reshape(2, 2, 2, 4, 16, WIDTH)

    def send_gin(i):
        p = lax.rem(station + i, 8)
        remote(
            gin_send.at[:, lax.rem(station + p, 2), :, p // 2], gin_recv.at[station], R_GIN,
            (dp, p, tm),
        )

    each(1, 8, send_gin)
    gin_recv[station] = gin_send[:, 0, :, y]

    for c in range(4):
        gain_send[0, c : c + 1, :] = gain_sum_s[:, 128 * c : 128 * c + 128]
        gain_send[0, 4 + c : 5 + c, :] = gain_sum_t[:, 128 * c : 128 * c + 128]

    def send_gain_s(i):
        p = lax.rem(station + i, 8)
        remote(gain_send.at[0], gain_s_recv.at[station], R_GAIN_S, (dp, p, tm))

    each(1, 8, send_gain_s)
    gain_s_recv[station] = gain_send[0]

    sums_own(0, ups_s[...])
    sums_first(0, R_STATION)
    sums_third(1, R_TIME)

    received(gain_s_recv.at[pl.ds(0, 7)], R_GAIN_S)
    value = gain_s_recv[0]
    for j in range(1, 8):
        value = value + gain_s_recv[j]
    gain_send[1] = value

    def send_gain_x(i):
        p = lax.rem(x_at + i, 4)
        remote(gain_send.at[1], gain_x_recv.at[x_at], R_GAIN_X, (dp, station, z_hi * 4 + p))

    each(1, 4, send_gain_x)
    gain_x_recv[x_at] = value
    sums_end(1, R_TIME)

    received(gain_x_recv.at[pl.ds(0, 3)], R_GAIN_X)
    value = gain_x_recv[0]
    for j in range(1, 4):
        value = value + gain_x_recv[j]
    gain_send[2] = value
    mine = 2 * z_hi + dp

    def send_gain_z(i):
        p = lax.rem(mine + i, 8)
        remote(
            gain_send.at[2], gain_z_recv.at[mine], R_GAIN_Z,
            (lax.rem(p, 2), station, (p // 2) * 4 + x_at),
        )

    each(1, 8, send_gain_z)
    gain_z_recv[mine] = value

    sums_second(0, R_STATION)

    received(gin_recv.at[pl.ds(0, 7)], R_GIN)
    for s in range(8):
        for e in range(2):
            for st in range(2):
                for c in range(4):
                    fine[c, pl.ds(st * 16 + 2 * s + e, 16, stride=32), :] = gin_recv[
                        s, e, st, :, 128 * c : 128 * c + 128
                    ].astype(F32)
    for c in range(4):
        gin_ref[:, :, 128 * c : 128 * c + 128] = fine[c].astype(BF).reshape(32, 16, 128)

    sums_third(0, R_STATION)
    received(gain_z_recv.at[pl.ds(0, 7)], R_GAIN_Z)
    value = gain_z_recv[0]
    for j in range(1, 8):
        value = value + gain_z_recv[j]
    gains_ref[...] = value

    sent(in_send.at[pl.ds(0, 7)], R_IN)
    sent(cot_recv.at[:, pl.ds(0, 15)], R_COT)
    for part in range(2):
        sent(mid_send.at[part, pl.ds(0, 63 + part)], R_MID + part)
        sent(gmid_send.at[part, pl.ds(0, 63 + part)], R_GMID + part)
    sent(gin_recv.at[pl.ds(0, 7)], R_GIN)
    sent(gain_s_recv.at[pl.ds(0, 7)], R_GAIN_S)
    sent(gain_x_recv.at[pl.ds(0, 3)], R_GAIN_X)
    sent(gain_z_recv.at[pl.ds(0, 7)], R_GAIN_Z)
    for layer, base in ((1, R_TIME), (0, R_STATION)):
        sent(pair_send.at[layer], base + PAIR)
        sent(y_recv.at[layer, pl.ds(0, 3)], base + FIRST_Y)
        sent(x1_recv.at[layer, pl.ds(0, 3)], base + FIRST_X)
        sent(xb_recv.at[layer, pl.ds(0, 3)], base + SECOND_X)
        sent(yb_recv.at[layer, pl.ds(0, 3)], base + SECOND_Y)
        sent(z_recv.at[layer, pl.ds(0, 7)], base + THIRD)
    sums_end(0, R_STATION)


def deliver(gin, sums, gains, gin_ref, gq_s_ref, go_s_ref, gg_s_ref, gq_t_ref, go_t_ref, gg_t_ref):
    gin_ref[...] = gin[...]
    for layer, qkv_ref, out_ref in ((0, gq_s_ref, go_s_ref), (1, gq_t_ref, go_t_ref)):
        value = sums[layer].astype(F32)
        qkv_ref[...] = value[:, 0:96].astype(BF)
        out_ref[...] = pltpu.roll(value, 32, 1)[:, 0:32].astype(BF)
    for c in range(4):
        gg_s_ref[:, 128 * c : 128 * c + 128] = gains[c : c + 1]
        gg_t_ref[:, 128 * c : 128 * c + 128] = gains[4 + c : 5 + c]


def local(inputs, cotangent, station_gain, station_qkv, station_out, time_gain, time_qkv, time_out):
    any_space = pl.BlockSpec(memory_space=pl.ANY)
    vmem = pl.BlockSpec(memory_space=pltpu.VMEM)
    shape = jax.ShapeDtypeStruct
    merged = pl.pallas_call(
        kernel,
        out_shape=(shape((32, 16, WIDTH), BF), shape((2, 64, 128), BF), shape((8, 128), F32)),
        in_specs=[any_space, any_space, vmem, any_space, any_space, vmem, any_space, any_space],
        out_specs=[vmem] * 3,
        scratch_shapes=[
            pltpu.VMEM((32, 16, WIDTH), BF),
            pltpu.VMEM((4, TOKENS, 128), F32),
            pltpu.VMEM((PEERS * 16, 128), F32),
            pltpu.VMEM((8, 2, 2, 16, WIDTH), BF),
            pltpu.VMEM((2, 2, 2, 4, 16, WIDTH), BF),
            pltpu.VMEM((2, 16, 16, WIDTH), BF),
            pltpu.VMEM((2, 2, 2, 4, 16, WIDTH), BF),
            pltpu.VMEM((WIDTH, 3 * WIDTH), BF),
            pltpu.VMEM((WIDTH, WIDTH), BF),
            pltpu.VMEM((WIDTH, 3 * WIDTH), BF),
            pltpu.VMEM((WIDTH, WIDTH), BF),
            pltpu.VMEM((2, TOKENS, WIDTH), BF),
            pltpu.VMEM((TOKENS, 3 * WIDTH), BF),
            pltpu.VMEM((TOKENS, 3 * WIDTH), BF),
            pltpu.VMEM((8, SEQ, 2 * SEQ), F32),
            pltpu.VMEM((2, TOKENS, WIDTH), BF),
            pltpu.VMEM((TOKENS, WIDTH), BF),
            pltpu.VMEM((TOKENS, 3 * WIDTH), BF),
            pltpu.VMEM((2, 4, 2, 64, TOKENS), BF),
            pltpu.VMEM((2, 4, 2, 64, TOKENS), BF),
            pltpu.VMEM((2, 64, 16, 128), BF),
            pltpu.VMEM((2, 64, 16, 128), BF),
            pltpu.VMEM((TOKENS, WIDTH), F32),
            pltpu.VMEM((2, 64, 16, 128), BF),
            pltpu.VMEM((2, 64, 16, 128), BF),
            pltpu.VMEM((TOKENS, WIDTH), BF),
            pltpu.VMEM((2, 2, 2, 4, 16, WIDTH), BF),
            pltpu.VMEM((8, 2, 2, 16, WIDTH), BF),
            pltpu.VMEM((4, 64, 4 * WIDTH), F32),
            pltpu.VMEM((2, 4, 64, 4 * WIDTH), BF),
            pltpu.VMEM((2, 4, 64, 4 * WIDTH), BF),
            pltpu.VMEM((2, 4, 16, 32, 128), BF),
            pltpu.VMEM((2, 4, 16, 32, 128), BF),
            pltpu.VMEM((2, 4, 4, 4, 32, 128), BF),
            pltpu.VMEM((2, 4, 4, 4, 32, 128), BF),
            pltpu.VMEM((2, 4, 4, 32, 128), BF),
            pltpu.VMEM((2, 4, 4, 32, 128), BF),
            pltpu.VMEM((2, 4, 4, 32, 128), BF),
            pltpu.VMEM((2, 4, 4, 32, 128), BF),
            pltpu.VMEM((2, 4, 64, 128), BF),
            pltpu.VMEM((2, 8, 64, 128), BF),
            pltpu.VMEM((3, 8, 128), F32),
            pltpu.VMEM((8, 8, 128), F32),
            pltpu.VMEM((4, 8, 128), F32),
            pltpu.VMEM((8, 8, 128), F32),
            pltpu.SemaphoreType.DMA((N_SEMS,)),
            pltpu.SemaphoreType.DMA((N_SEMS,)),
            pltpu.SemaphoreType.DMA((6,)),
        ],
        compiler_params=pltpu.CompilerParams(
            collective_id=0, has_side_effects=True, vmem_limit_bytes=60 * 2**20
        ),
    )(
        inputs.reshape(32, 16, WIDTH), cotangent.reshape(32, 16, WIDTH),
        station_gain.reshape(1, WIDTH), station_qkv, station_out,
        time_gain.reshape(1, WIDTH), time_qkv, time_out,
    )
    grad_in, qkv_s, out_s, gain_s, qkv_t, out_t, gain_t = pl.pallas_call(
        deliver,
        out_shape=(
            shape((32, 16, WIDTH), BF),
            shape((64, 96), BF), shape((64, 32), BF), shape((1, WIDTH), F32),
            shape((64, 96), BF), shape((64, 32), BF), shape((1, WIDTH), F32),
        ),
        in_specs=[vmem] * 3,
        out_specs=[vmem] * 7,
    )(*merged)
    return (
        grad_in.reshape(inputs.shape),
        qkv_s, out_s, gain_s.reshape(WIDTH), qkv_t, out_t, gain_t.reshape(WIDTH),
    )


def solution(mesh):
    rows = P("dp", "station", "tm", None)
    split = P("station", "tm")
    return jax.shard_map(
        local,
        mesh=mesh,
        in_specs=(rows, rows, P(), P(), P(), P(), P(), P()),
        out_specs=(rows, split, split, P(), split, split, P()),
        check_vma=False,
    )
```

time: 124 us -> 94.8 us (0.76); the launches traced: 122 us -> 94.5 us
  Pallas kernels: 112 us -> 91 us
  local copies, waits for them, and re-layouts: 9.79 us -> 2.78 us
    pallas_call x1 -> x2, Pallas kernels: 112 us -> 91 us  [the longest x1 89.1 us: local(): pl.pallas_call(kernel, out_shape=(shape((32, 16, WIDTH), BF), shape((2, 6...]
    unnamed x7 -> x2, local copies, waits for them, and re-layouts: 9.79 us -> 2.78 us
where the time goes in v2:
time: 94.8 us; the launch traced here: 94.5 us
  Pallas kernels  91 us (96%)
  local copies, waits for them, and re-layouts  2.78 us (3%)
    pallas_call x1, Pallas kernels, local(): pl.pallas_call(kernel, out_shape=(shape((32, 16, WIDTH), BF), shape((2, 6...  89.1 us
    unnamed x2, local copies, waits for them, and re-layouts  2.78 us
    pallas_call x1, Pallas kernels, local(): pl.pallas_call(deliver, out_shape=(shape((32, 16, WIDTH), BF), shape((64,...  1.91 us

profile of v2, /device:TPU:6, one launch (start us, length us, event | category | flops | bytes accessed | tf_op | source)
XLA Modules:
  0.0 94.5 jit_solution(14381775072705680677)
XLA Ops:
  0.6 89.1 %shard_map.135 = (bf16[32,16,512]{2,1,0:T(8,128)(2,1)}, bf16[2,64,128]{2,1,0:T(8,128)(2,1)}, f32[8,128]{1,0:T(8,128)}) custom-call(bf16[32,16,512]{2,1,0:T(8,128)(2,1)} %bitcast.7, bf16[32,16,512]{2,1,0:T(8,128)(2,1)} %bitcast.8, f32[1,512]{1,0:T(1,128)} %bitcast.9, bf16[512,1536]{1,0:T(8,128)(2,1)} %wq_s_hbm.1, bf16[512,512]{1,0:T(8,128)(2,1)} %wo_s_hbm.1, ...), custom_call_target="tpu_custom_call" | custom-call | tf_op jit(solution)/shard_map/pallas_call | solution.py:587
  89.8 1.9 %shard_map.136 = (bf16[32,16,512]{2,1,0:T(8,128)(2,1)}, bf16[64,96]{1,0:T(8,128)(2,1)}, bf16[64,32]{1,0:T(8,128)(2,1)}, f32[1,512]{1,0:T(1,128)}, bf16[64,96]{1,...) custom-call(bf16[32,16,512]{2,1,0:T(8,128)(2,1)} %get-tuple-element.17.gin, ...), custom_call_target="tpu_custom_call" | custom-call | tf_op jit(solution)/shard_map/pallas_call | solution.py:650
  91.7 1.4 %copy.15 = bf16[64,32]{0,1:T(8,128)(2,1)} copy(bf16[64,32]{1,0:T(8,128)(2,1)} %get-tuple-element.29) | data formatting | bytes 8192
  93.1 1.4 %copy.16 = bf16[64,32]{0,1:T(8,128)(2,1)} copy(bf16[64,32]{1,0:T(8,128)(2,1)} %get-tuple-element.32) | data formatting | bytes 8192

commit v3 on v2

--- a/solution.py
+++ b/solution.py
@@ -21,8 +21,9 @@
     0, 1, 2, 3, 4, 5, 6, 8, 10, 16,
 )
 PAIR, FIRST_Y, FIRST_X, SECOND_X, SECOND_Y, THIRD = range(6)
-N_SEMS = 22
-L_X, L_COT, L_WQS, L_WOS, L_WQT, L_WOT = range(6)
+FIRST_Z, Z_THEN_Y, Z_THEN_X = 6, 7, 8
+N_SEMS = 25
+L_X, L_COT, L_WQS, L_WOS, L_WQT, L_WOT, L_OUT = range(7)
 CHUNK = 128
 
 
@@ -110,6 +111,31 @@
     ).astype(BF)
 
 
+def turn(value, by):
+    return pltpu.roll(value, by, 1)
+
+
+def slot(t, piece):
+    lane = lax.broadcasted_iota(jnp.int32, (1, 128), 1)
+    j, i = t // 4, t % 4
+    parts = {
+        0: ((3 * j, 0, 0, 96),),
+        1: ((3 * j, 32, 0, 32), (3 * j + 1, 32, 32, 96)),
+        2: ((3 * j + 1, 64, 0, 64), (3 * j + 2, 64, 64, 96)),
+        3: ((3 * j + 2, 96, 0, 96),),
+    }[i] + ((12 + j, 96 - 32 * i, 96, 128),)
+    result = None
+    for at, by, first, last in parts:
+        value = piece(at)
+        if value is None:
+            continue
+        if by:
+            value = turn(value, by)
+        inside = (lane >= first) & (lane < last)
+        result = jnp.where(inside, value, 0.0 if result is None else result)
+    return result
+
+
 def normalise(x, gain):
     inverse = lax.rsqrt(jnp.mean(x * x, axis=1, keepdims=True) + EPSILON)
     normed = x * inverse
@@ -161,12 +187,14 @@
 
 def kernel(
     x_hbm, cot_hbm, gain_s_ref, wq_s_hbm, wo_s_hbm, gain_t_ref, wq_t_hbm, wo_t_hbm,
-    gin_ref, sums_ref, gains_ref,
+    gin_hbm, sums_ref, gains_ref,
     x_raw, fine, wide, in_send, xs, cot_recv, ups_t, wq_s, wo_s, wq_t, wo_t,
     acted, joined_s, joined_t, probs, attended, grad_att, grad_joined, acted_t, att_t,
     mid_send, mid_recv, xt, gmid_send, gmid_recv, ups_s, gin_send, gin_recv,
     total, pair_send, pair_recv, y_send, y_recv, x1_send, x1_recv,
     xb_send, xb_recv, yb_send, yb_recv, z_send, z_recv,
+    sy_send, sy_recv, sx_send, sx_recv, sz_send, sz_recv, syx_send, syx_recv, sxy_send, sxy_recv,
+    szy_send, szy_recv, szx_send, szx_recv, s_send, s_recv,
     gain_send, gain_s_recv, gain_x_recv, gain_z_recv,
     send_sems, recv_sems, local_sems,
 ):
@@ -216,6 +244,7 @@
     each(1, 8, lambda i: greet((dp, lax.rem(station + i, 8), tm)))
     each(1, 16, lambda i: greet((dp, station, lax.rem(tm + i, 16))))
     each(0, 4, lambda i: greet((1 - dp, station, i * 4 + x_at)))
+    each(1, 4, lambda i: greet((1 - dp, station, z_hi * 4 + lax.rem(x_at + i, 4))))
 
     loads[0].wait()
     for c in range(4):
@@ -227,7 +256,7 @@
                     in_send[s, e, st, :, 128 * c : 128 * c + 128] = fine[
                         c, pl.ds(st * 16 + 2 * s + e, 16, stride=32), :
                     ].astype(BF)
-    pl.semaphore_wait(barrier, 26)
+    pl.semaphore_wait(barrier, 29)
 
     def send_in(i):
         p = lax.rem(station + i, 8)
@@ -342,7 +371,6 @@
 
     def sums_first(layer, base):
         received(pair_recv.at[layer], base + PAIR)
-        lane = lax.broadcasted_iota(jnp.int32, (1, 128), 1)
 
         def fill(i):
             def put(t, value):
@@ -350,17 +378,12 @@
                 y_send[layer, i, t] = value[0:32]
                 x1_send[layer, t % 4, i, t // 4] = value[32:64]
 
-            for j in range(4):
-                def piece(at):
-                    where = slice(at * 128, at * 128 + 128)
-                    return total[i, :, where] + pair_recv[layer, i, :, where].astype(F32)
-
-                a, b, c, o = piece(3 * j), piece(3 * j + 1), piece(3 * j + 2), piece(12 + j)
-                turn = lambda v, by: pltpu.roll(v, by, 1)
-                put(4 * j, jnp.where(lane < 96, a, turn(o, 96)))
-                put(4 * j + 1, jnp.where(lane < 32, turn(a, 32), jnp.where(lane < 96, turn(b, 32), turn(o, 64))))
-                put(4 * j + 2, jnp.where(lane < 64, turn(b, 64), jnp.where(lane < 96, turn(c, 64), turn(o, 32))))
-                put(4 * j + 3, jnp.where(lane < 96, turn(c, 96), o))
+            def piece(at):
+                where = slice(at * 128, at * 128 + 128)
+                return total[i, :, where] + pair_recv[layer, i, :, where].astype(F32)
+
+            for t in range(16):
+                put(t, slot(t, piece))
 
         each(0, 4, fill)
 
@@ -451,6 +474,114 @@
             value = value + z_recv[layer, j].astype(F32)
         sums_ref[layer] = value.astype(BF)
 
+    def along(send, recv, sem, mine, device):
+        def action(i):
+            p = lax.rem(mine + i, 4)
+            remote(send.at[p], recv.at[mine], R_STATION + sem, device(p))
+
+        each(1, 4, action)
+        recv[mine] = send[mine]
+
+    def at_y(p):
+        return (dp, 2 * p + core, tm)
+
+    def at_x(p):
+        return (dp, station, z_hi * 4 + p)
+
+    def at_z(p):
+        return (dp, station, p * 4 + x_at)
+
+    def gathered(recv, sem):
+        received(recv.at[pl.ds(0, recv.shape[0] - 1)], R_STATION + sem)
+
+    def summed(recv, *where):
+        value = recv[(0,) + where].astype(F32)
+        for j in range(1, recv.shape[0]):
+            value = value + recv[(j,) + where].astype(F32)
+        return value
+
+    def station_first():
+        received(pair_recv.at[0], R_STATION + PAIR)
+
+        def fill(i):
+            def piece(at):
+                where = slice(at * 128, at * 128 + 128)
+                return total[i, :, where] + pair_recv[0, i, :, where].astype(F32)
+
+            for t in range(16):
+                value = slot(t, piece).astype(BF)
+                sy_send[i, t] = value[0:16]
+                sz_send[t // 4, t % 4, i] = value[16:32]
+                sx_send[t % 4, i, t // 4] = value[32:64]
+
+        each(0, 4, fill)
+        along(sz_send, sz_recv, FIRST_Z, z_hi, at_z)
+        along(sx_send, sx_recv, FIRST_X, x_at, at_x)
+        along(sy_send, sy_recv, FIRST_Y, y, at_y)
+
+    def station_second():
+        gathered(sy_recv, FIRST_Y)
+
+        def add_y(i):
+            for at in range(4):
+                syx_send[at, i] = summed(sy_recv, 4 * i + at).astype(BF)
+
+        each(0, 4, add_y)
+        along(syx_send, syx_recv, SECOND_X, x_at, at_x)
+        gathered(sz_recv, FIRST_Z)
+
+        def add_z(i):
+            for at in range(4):
+                szy_send[i, at] = summed(sz_recv, at, i).astype(BF)
+
+        each(0, 4, add_z)
+        along(szy_send, szy_recv, Z_THEN_Y, y, at_y)
+        gathered(sx_recv, FIRST_X)
+
+        def add_x(i):
+            sxy_send[i] = summed(sx_recv, i).astype(BF)
+
+        each(0, 4, add_x)
+        along(sxy_send, sxy_recv, SECOND_Y, y, at_y)
+
+    def station_third():
+        gathered(szy_recv, Z_THEN_Y)
+        szx_send[...] = summed(szy_recv).astype(BF)
+        mine_x = 2 * x_at + dp
+
+        def send_x(i):
+            p = lax.rem(mine_x + i, 8)
+            remote(
+                szx_send.at[p // 2], szx_recv.at[mine_x], R_STATION + Z_THEN_X,
+                (lax.rem(p, 2), station, z_hi * 4 + p // 2),
+            )
+
+        each(1, 8, send_x)
+        szx_recv[mine_x] = szx_send[x_at]
+        gathered(syx_recv, SECOND_X)
+        s_send[:, 0:16] = summed(syx_recv).astype(BF)
+        gathered(sxy_recv, SECOND_Y)
+        s_send[:, 16:48] = summed(sxy_recv).astype(BF)
+        mine_z = 2 * z_hi + dp
+
+        def send_z(i):
+            p = lax.rem(mine_z + i, 8)
+            remote(
+                s_send.at[p // 2], s_recv.at[mine_z], R_STATION + THIRD,
+                (lax.rem(p, 2), station, (p // 2) * 4 + x_at),
+            )
+
+        each(1, 8, send_z)
+        s_recv[mine_z] = s_send[z_hi]
+
+    def station_end():
+        gathered(szx_recv, Z_THEN_X)
+        sums_ref[0, 16:32] = summed(szx_recv).astype(BF)
+        gathered(s_recv, THIRD)
+        value = summed(s_recv).astype(BF)
+        sums_ref[0, 0:16] = value[0:16]
+        sums_ref[0, 32:64] = value[16:48]
+
     acted_t[1] = acted[1].T.reshape(4, 2, 64, TOKENS)
     att_t[1] = attended[1].T.reshape(4, 2, 64, TOKENS)
     sums_send(1, R_TIME, upstream_t)
@@ -465,7 +596,7 @@
         for pair in range(PAIRS):
             backward_step(seq, pair, joined_s, probs, None, grad_att, grad_joined)
     sums_send(0, R_STATION, ups_s[...])
-    sums_second(1, R_TIME)
+    sums_own(0, ups_s[...])
     grad_acted = nt(grad_joined[...], wq_s[...])
     x_value = xs[...].reshape(TOKENS, WIDTH).astype(F32)
     inverse_s = lax.rsqrt(jnp.mean(x_value * x_value, axis=1, keepdims=True) + EPSILON)
@@ -473,6 +604,7 @@
         x_value, inverse_s, gain_s, grad_acted, ups_s[...].astype(F32)
     )
     gin_send[...] = grad_in.astype(BF).reshape(2, 2, 2, 4, 16, WIDTH)
+    station_first()
 
     def send_gin(i):
         p = lax.rem(station + i, 8)
@@ -495,9 +627,7 @@
     each(1, 8, send_gain_s)
     gain_s_recv[station] = gain_send[0]
 
-    sums_own(0, ups_s[...])
-    sums_first(0, R_STATION)
-    sums_third(1, R_TIME)
+    sums_second(1, R_TIME)
 
     received(gain_s_recv.at[pl.ds(0, 7)], R_GAIN_S)
     value = gain_s_recv[0]
@@ -511,7 +641,8 @@
 
     each(1, 4, send_gain_x)
     gain_x_recv[x_at] = value
-    sums_end(1, R_TIME)
+    station_second()
+    sums_third(1, R_TIME)
 
     received(gain_x_recv.at[pl.ds(0, 3)], R_GAIN_X)
     value = gain_x_recv[0]
@@ -530,7 +661,7 @@
     each(1, 8, send_gain_z)
     gain_z_recv[mine] = value
 
-    sums_second(0, R_STATION)
+    station_third()
 
     received(gin_recv.at[pl.ds(0, 7)], R_GIN)
     for s in range(8):
@@ -541,9 +672,11 @@
                         s, e, st, :, 128 * c : 128 * c + 128
                     ].astype(F32)
     for c in range(4):
-        gin_ref[:, :, 128 * c : 128 * c + 128] = fine[c].astype(BF).reshape(32, 16, 128)
-
-    sums_third(0, R_STATION)
+        x_raw[:, :, 128 * c : 128 * c + 128] = fine[c].astype(BF).reshape(32, 16, 128)
+    result = local_copy(x_raw, gin_hbm, L_OUT)
+    result.start()
+
+    sums_end(1, R_TIME)
     received(gain_z_recv.at[pl.ds(0, 7)], R_GAIN_Z)
     value = gain_z_recv[0]
     for j in range(1, 8):
@@ -559,14 +692,20 @@
     sent(gain_s_recv.at[pl.ds(0, 7)], R_GAIN_S)
     sent(gain_x_recv.at[pl.ds(0, 3)], R_GAIN_X)
     sent(gain_z_recv.at[pl.ds(0, 7)], R_GAIN_Z)
-    for layer, base in ((1, R_TIME), (0, R_STATION)):
-        sent(pair_send.at[layer], base + PAIR)
-        sent(y_recv.at[layer, pl.ds(0, 3)], base + FIRST_Y)
-        sent(x1_recv.at[layer, pl.ds(0, 3)], base + FIRST_X)
-        sent(xb_recv.at[layer, pl.ds(0, 3)], base + SECOND_X)
-        sent(yb_recv.at[layer, pl.ds(0, 3)], base + SECOND_Y)
-        sent(z_recv.at[layer, pl.ds(0, 7)], base + THIRD)
-    sums_end(0, R_STATION)
+    sent(pair_send.at[1], R_TIME + PAIR)
+    sent(y_recv.at[1, pl.ds(0, 3)], R_TIME + FIRST_Y)
+    sent(x1_recv.at[1, pl.ds(0, 3)], R_TIME + FIRST_X)
+    sent(xb_recv.at[1, pl.ds(0, 3)], R_TIME + SECOND_X)
+    sent(yb_recv.at[1, pl.ds(0, 3)], R_TIME + SECOND_Y)
+    sent(z_recv.at[1, pl.ds(0, 7)], R_TIME + THIRD)
+    sent(pair_send.at[0], R_STATION + PAIR)
+    for recv, sem in (
+        (sy_recv, FIRST_Y), (sx_recv, FIRST_X), (sz_recv, FIRST_Z), (syx_recv, SECOND_X),
+        (sxy_recv, SECOND_Y), (szy_recv, Z_THEN_Y), (szx_recv, Z_THEN_X), (s_recv, THIRD),
+    ):
+        sent(recv.at[pl.ds(0, recv.shape[0] - 1)], R_STATION + sem)
+    station_end()
+    result.wait()
 
 
 def deliver(gin, sums, gains, gin_ref, gq_s_ref, go_s_ref, gg_s_ref, gq_t_ref, go_t_ref, gg_t_ref):
@@ -574,7 +713,7 @@
     for layer, qkv_ref, out_ref in ((0, gq_s_ref, go_s_ref), (1, gq_t_ref, go_t_ref)):
         value = sums[layer].astype(F32)
         qkv_ref[...] = value[:, 0:96].astype(BF)
-        out_ref[...] = pltpu.roll(value, 32, 1)[:, 0:32].astype(BF)
+        out_ref[...] = value.T[96:128].astype(BF)
     for c in range(4):
         gg_s_ref[:, 128 * c : 128 * c + 128] = gains[c : c + 1]
         gg_t_ref[:, 128 * c : 128 * c + 128] = gains[4 + c : 5 + c]
@@ -588,7 +727,7 @@
         kernel,
         out_shape=(shape((32, 16, WIDTH), BF), shape((2, 64, 128), BF), shape((8, 128), F32)),
         in_specs=[any_space, any_space, vmem, any_space, any_space, vmem, any_space, any_space],
-        out_specs=[vmem] * 3,
+        out_specs=[any_space, vmem, vmem],
         scratch_shapes=[
             pltpu.VMEM((32, 16, WIDTH), BF),
             pltpu.VMEM((4, TOKENS, 128), F32),
@@ -631,13 +770,29 @@
             pltpu.VMEM((2, 4, 4, 32, 128), BF),
             pltpu.VMEM((2, 4, 64, 128), BF),
             pltpu.VMEM((2, 8, 64, 128), BF),
+            pltpu.VMEM((4, 16, 16, 128), BF),
+            pltpu.VMEM((4, 16, 16, 128), BF),
+            pltpu.VMEM((4, 4, 4, 32, 128), BF),
+            pltpu.VMEM((4, 4, 4, 32, 128), BF),
+            pltpu.VMEM((4, 4, 4, 16, 128), BF),
+            pltpu.VMEM((4, 4, 4, 16, 128), BF),
+            pltpu.VMEM((4, 4, 16, 128), BF),
+            pltpu.VMEM((4, 4, 16, 128), BF),
+            pltpu.VMEM((4, 4, 32, 128), BF),
+            pltpu.VMEM((4, 4, 32, 128), BF),
+            pltpu.VMEM((4, 4, 16, 128), BF),
+            pltpu.VMEM((4, 4, 16, 128), BF),
+            pltpu.VMEM((4, 16, 128), BF),
+            pltpu.VMEM((8, 16, 128), BF),
+            pltpu.VMEM((4, 48, 128), BF),
+            pltpu.VMEM((8, 48, 128), BF),
             pltpu.VMEM((3, 8, 128), F32),
             pltpu.VMEM((8, 8, 128), F32),
             pltpu.VMEM((4, 8, 128), F32),
             pltpu.VMEM((8, 8, 128), F32),
             pltpu.SemaphoreType.DMA((N_SEMS,)),
             pltpu.SemaphoreType.DMA((N_SEMS,)),
-            pltpu.SemaphoreType.DMA((6,)),
+            pltpu.SemaphoreType.DMA((7,)),
         ],
         compiler_params=pltpu.CompilerParams(
             collective_id=0, has_side_effects=True, vmem_limit_bytes=60 * 2**20
@@ -651,15 +806,15 @@
         deliver,
         out_shape=(
             shape((32, 16, WIDTH), BF),
-            shape((64, 96), BF), shape((64, 32), BF), shape((1, WIDTH), F32),
-            shape((64, 96), BF), shape((64, 32), BF), shape((1, WIDTH), F32),
+            shape((64, 96), BF), shape((32, 64), BF), shape((1, WIDTH), F32),
+            shape((64, 96), BF), shape((32, 64), BF), shape((1, WIDTH), F32),
         ),
         in_specs=[vmem] * 3,
         out_specs=[vmem] * 7,
     )(*merged)
     return (
         grad_in.reshape(inputs.shape),
-        qkv_s, out_s, gain_s.reshape(WIDTH), qkv_t, out_t, gain_t.reshape(WIDTH),
+        qkv_s, out_s.T, gain_s.reshape(WIDTH), qkv_t, out_t.T, gain_t.reshape(WIDTH),
     )
 
 

time: 94.8 us -> 92.6 us (0.977)
  local copies, waits for them, and re-layouts: 2.78 us -> 0 us
    unnamed x2 -> x0, local copies, waits for them, and re-layouts: 2.78 us -> none
where the time goes in v3:
time: 92.6 us; the launch traced here: 91.9 us
  Pallas kernels  91.3 us (99%)
    pallas_call x1, Pallas kernels, local(): pl.pallas_call(kernel, out_shape=(shape((32, 16, WIDTH), BF), shape((2, 6...  89.4 us
    pallas_call x1, Pallas kernels, local(): pl.pallas_call(deliver, out_shape=(shape((32, 16, WIDTH), BF), shape((64,...  1.91 us

profile of v3, /device:TPU:6, one launch (start us, length us, event | category | flops | bytes accessed | tf_op | source)
XLA Modules:
  0.0 91.9 jit_solution(1330659840516614816)
XLA Ops:
  0.6 89.4 %shard_map.135 = (bf16[32,16,512]{2,1,0:T(8,128)(2,1)}, bf16[2,64,128]{2,1,0:T(8,128)(2,1)}, f32[8,128]{1,0:T(8,128)}) custom-call(bf16[32,16,512]{2,1,0:T(8,128)(2,1)} %bitcast.9, bf16[32,16,512]{2,1,0:T(8,128)(2,1)} %bitcast.10, f32[1,512]{1,0:T(1,128)} %bitcast.11, bf16[512,1536]{1,0:T(8,128)(2,1)} %wq_s_hbm.1, bf16[512,512]{1,0:T(8,128)(2,1)} %wo_s_hbm.1, ...), custom_call_target="tpu_custom_call" | custom-call | tf_op jit(solution)/shard_map/pallas_call | solution.py:726
  90.0 1.9 %shard_map.136 = (bf16[32,16,512]{2,1,0:T(8,128)(2,1)}, bf16[64,96]{1,0:T(8,128)(2,1)}, bf16[32,64]{1,0:T(8,128)(2,1)}, f32[1,512]{1,0:T(1,128)}, bf16[64,96]{1,...) custom-call(bf16[32,16,512]{2,1,0:T(8,128)(2,1)} %get-tuple-element.17.gin, ...), custom_call_target="tpu_custom_call" | custom-call | tf_op jit(solution)/shard_map/pallas_call | solution.py:805

commit v4 on v2

--- a/solution.py
+++ b/solution.py
@@ -22,7 +22,7 @@
 )
 PAIR, FIRST_Y, FIRST_X, SECOND_X, SECOND_Y, THIRD = range(6)
 N_SEMS = 22
-L_X, L_COT, L_WQS, L_WOS, L_WQT, L_WOT = range(6)
+L_X, L_COT, L_WQS, L_WOS, L_WQT, L_WOT, L_OUT = range(7)
 CHUNK = 128
 
 
@@ -161,7 +161,7 @@
 
 def kernel(
     x_hbm, cot_hbm, gain_s_ref, wq_s_hbm, wo_s_hbm, gain_t_ref, wq_t_hbm, wo_t_hbm,
-    gin_ref, sums_ref, gains_ref,
+    gin_hbm, sums_ref, gains_ref,
     x_raw, fine, wide, in_send, xs, cot_recv, ups_t, wq_s, wo_s, wq_t, wo_t,
     acted, joined_s, joined_t, probs, attended, grad_att, grad_joined, acted_t, att_t,
     mid_send, mid_recv, xt, gmid_send, gmid_recv, ups_s, gin_send, gin_recv,
@@ -541,7 +541,9 @@
                         s, e, st, :, 128 * c : 128 * c + 128
                     ].astype(F32)
     for c in range(4):
-        gin_ref[:, :, 128 * c : 128 * c + 128] = fine[c].astype(BF).reshape(32, 16, 128)
+        x_raw[:, :, 128 * c : 128 * c + 128] = fine[c].astype(BF).reshape(32, 16, 128)
+    result = local_copy(x_raw, gin_hbm, L_OUT)
+    result.start()
 
     sums_third(0, R_STATION)
     received(gain_z_recv.at[pl.ds(0, 7)], R_GAIN_Z)
@@ -567,6 +569,7 @@
         sent(yb_recv.at[layer, pl.ds(0, 3)], base + SECOND_Y)
         sent(z_recv.at[layer, pl.ds(0, 7)], base + THIRD)
     sums_end(0, R_STATION)
+    result.wait()
 
 
 def deliver(gin, sums, gains, gin_ref, gq_s_ref, go_s_ref, gg_s_ref, gq_t_ref, go_t_ref, gg_t_ref):
@@ -574,7 +577,7 @@
     for layer, qkv_ref, out_ref in ((0, gq_s_ref, go_s_ref), (1, gq_t_ref, go_t_ref)):
         value = sums[layer].astype(F32)
         qkv_ref[...] = value[:, 0:96].astype(BF)
-        out_ref[...] = pltpu.roll(value, 32, 1)[:, 0:32].astype(BF)
+        out_ref[...] = value.T[96:128].astype(BF)
     for c in range(4):
         gg_s_ref[:, 128 * c : 128 * c + 128] = gains[c : c + 1]
         gg_t_ref[:, 128 * c : 128 * c + 128] = gains[4 + c : 5 + c]
@@ -588,7 +591,7 @@
         kernel,
         out_shape=(shape((32, 16, WIDTH), BF), shape((2, 64, 128), BF), shape((8, 128), F32)),
         in_specs=[any_space, any_space, vmem, any_space, any_space, vmem, any_space, any_space],
-        out_specs=[vmem] * 3,
+        out_specs=[any_space, vmem, vmem],
         scratch_shapes=[
             pltpu.VMEM((32, 16, WIDTH), BF),
             pltpu.VMEM((4, TOKENS, 128), F32),
@@ -637,7 +640,7 @@
             pltpu.VMEM((8, 8, 128), F32),
             pltpu.SemaphoreType.DMA((N_SEMS,)),
             pltpu.SemaphoreType.DMA((N_SEMS,)),
-            pltpu.SemaphoreType.DMA((6,)),
+            pltpu.SemaphoreType.DMA((7,)),
         ],
         compiler_params=pltpu.CompilerParams(
             collective_id=0, has_side_effects=True, vmem_limit_bytes=60 * 2**20
@@ -651,15 +654,15 @@
         deliver,
         out_shape=(
             shape((32, 16, WIDTH), BF),
-            shape((64, 96), BF), shape((64, 32), BF), shape((1, WIDTH), F32),
-            shape((64, 96), BF), shape((64, 32), BF), shape((1, WIDTH), F32),
+            shape((64, 96), BF), shape((32, 64), BF), shape((1, WIDTH), F32),
+            shape((64, 96), BF), shape((32, 64), BF), shape((1, WIDTH), F32),
         ),
         in_specs=[vmem] * 3,
         out_specs=[vmem] * 7,
     )(*merged)
     return (
         grad_in.reshape(inputs.shape),
-        qkv_s, out_s, gain_s.reshape(WIDTH), qkv_t, out_t, gain_t.reshape(WIDTH),
+        qkv_s, out_s.T, gain_s.reshape(WIDTH), qkv_t, out_t.T, gain_t.reshape(WIDTH),
     )
 
 

time: 94.8 us -> 91.7 us (0.967)
  local copies, waits for them, and re-layouts: 2.78 us -> 0 us
    unnamed x2 -> x0, local copies, waits for them, and re-layouts: 2.78 us -> none
where the time goes in v4:
time: 91.7 us; the launch traced here: 91.5 us
  Pallas kernels  90.9 us (99%)
    pallas_call x1, Pallas kernels, local(): pl.pallas_call(kernel, out_shape=(shape((32, 16, WIDTH), BF), shape((2, 6...  89 us
    pallas_call x1, Pallas kernels, local(): pl.pallas_call(deliver, out_shape=(shape((32, 16, WIDTH), BF), shape((64,...  1.91 us

profile of v4, /device:TPU:6, one launch (start us, length us, event | category | flops | bytes accessed | tf_op | source)
XLA Modules:
  0.0 91.5 jit_solution(6380413601300443073)
XLA Ops:
  0.6 89.0 %shard_map.135 = (bf16[32,16,512]{2,1,0:T(8,128)(2,1)}, bf16[2,64,128]{2,1,0:T(8,128)(2,1)}, f32[8,128]{1,0:T(8,128)}) custom-call(bf16[32,16,512]{2,1,0:T(8,128)(2,1)} %bitcast.9, bf16[32,16,512]{2,1,0:T(8,128)(2,1)} %bitcast.10, f32[1,512]{1,0:T(1,128)} %bitcast.11, bf16[512,1536]{1,0:T(8,128)(2,1)} %wq_s_hbm.1, bf16[512,512]{1,0:T(8,128)(2,1)} %wo_s_hbm.1, ...), custom_call_target="tpu_custom_call" | custom-call | tf_op jit(solution)/shard_map/pallas_call | solution.py:590
  89.6 1.9 %shard_map.136 = (bf16[32,16,512]{2,1,0:T(8,128)(2,1)}, bf16[64,96]{1,0:T(8,128)(2,1)}, bf16[32,64]{1,0:T(8,128)(2,1)}, f32[1,512]{1,0:T(1,128)}, bf16[64,96]{1,...) custom-call(bf16[32,16,512]{2,1,0:T(8,128)(2,1)} %get-tuple-element.17.gin, ...), custom_call_target="tpu_custom_call" | custom-call | tf_op jit(solution)/shard_map/pallas_call | solution.py:653

commit v5 on v4

--- a/solution.py
+++ b/solution.py
@@ -21,7 +21,9 @@
     0, 1, 2, 3, 4, 5, 6, 8, 10, 16,
 )
 PAIR, FIRST_Y, FIRST_X, SECOND_X, SECOND_Y, THIRD = range(6)
-N_SEMS = 22
+R_INS = (R_IN, 22)
+R_COTS = (R_COT, 23)
+N_SEMS = 24
 L_X, L_COT, L_WQS, L_WOS, L_WQT, L_WOT, L_OUT = range(7)
 CHUNK = 128
 
@@ -229,27 +231,40 @@
                     ].astype(BF)
     pl.semaphore_wait(barrier, 26)
 
-    def send_in(i):
-        p = lax.rem(station + i, 8)
-        remote(
-            in_send.at[p], xs.at[:, lax.rem(station + p, 2), :, y], R_IN, (dp, p, tm)
-        )
-
-    def send_cot(i):
-        p = lax.rem(tm + i, 16)
-        remote(cot_hbm.at[pl.ds(2 * p, 2)], cot_recv.at[:, tm], R_COT, (dp, station, p))
-
-    each(1, 8, send_in)
-    each(1, 16, send_cot)
+    def send_in(e):
+        def action(i):
+            p = lax.rem(station + i, 8)
+            remote(
+                in_send.at[p, e], xs.at[e, lax.rem(station + p, 2), :, y], R_INS[e], (dp, p, tm)
+            )
+
+        each(1, 8, action)
+
+    def send_cot(st):
+        def action(i):
+            p = lax.rem(tm + i, 16)
+            remote(cot_hbm.at[2 * p + st], cot_recv.at[st, tm], R_COTS[st], (dp, station, p))
+
+        each(1, 16, action)
+
+    send_in(0)
+    send_in(1)
+    send_cot(0)
     xs[:, 0, :, y] = in_send[station]
 
-    received(in_send.at[pl.ds(0, 7)], R_IN)
     loads[1].wait()
+    loads[2].wait()
     gain_s = gain_s_ref[...]
-    _, acted_value = normalise(xs[...].reshape(TOKENS, WIDTH).astype(F32), gain_s)
-    acted[0] = acted_value
-    joined_s[...] = nn(acted_value, wq_s[...]).astype(BF)
-    loads[2].wait()
+    for seq in range(2):
+        received(in_send.at[pl.ds(0, 7), seq], R_INS[seq])
+        rows = slice(seq * SEQ, seq * SEQ + SEQ)
+        _, acted_value = normalise(xs[seq].reshape(SEQ, WIDTH).astype(F32), gain_s)
+        acted[0, rows] = acted_value
+        joined_s[rows] = nn(acted_value, wq_s[...]).astype(BF)
+        if seq == 0:
+            for part in range(2):
+                for pair in range(PAIRS):
+                    forward_part(0, pair, part, joined_s, probs, attended.at[0])
 
     def send_parts(send, recv, sem, part):
         other = lax.rem(core + part, 2)
@@ -264,9 +279,8 @@
         each(1 - part, 64, action)
 
     for part in range(2):
-        for seq in range(2):
-            for pair in range(PAIRS):
-                forward_part(seq, pair, part, joined_s, probs, attended.at[0])
+        for pair in range(PAIRS):
+            forward_part(1, pair, part, joined_s, probs, attended.at[0])
         x_part = jnp.concatenate(
             [xs[0, part].reshape(128, WIDTH), xs[1, part].reshape(128, WIDTH)], axis=0
         )
@@ -275,22 +289,26 @@
         send_parts(mid_send, mid_recv, R_MID, part)
     mid_recv[0, spot] = mid_send[0, spot]
 
-    loads[3].wait()
-    received(cot_recv.at[:, pl.ds(0, 15)], R_COT)
-    for c in range(4):
-        fine[c] = cot_recv[:, :, :, 128 * c : 128 * c + 128].astype(F32).reshape(TOKENS, 128)
-    for s in range(8):
-        part = lax.rem(core + s, 2)
-        for st in range(2):
+    send_cot(1)
+
+    def take_cot(st):
+        received(cot_recv.at[st, pl.ds(0, 15)], R_COTS[st])
+        for c in range(4):
+            fine[c, 0:SEQ] = cot_recv[st, :, :, 128 * c : 128 * c + 128].astype(F32).reshape(SEQ, 128)
+        for s in range(8):
+            part = lax.rem(core + s, 2)
             for e in range(2):
                 for c in range(4):
                     ups_t[st, part, e, s // 2, :, 128 * c : 128 * c + 128] = fine[
-                        c, pl.ds(st * 256 + 2 * s + e, 16, stride=16), :
+                        c, pl.ds(2 * s + e, 16, stride=16), :
                     ].astype(BF)
-    loads[4].wait()
-    loads[5].wait()
-    upstream_t = ups_t[...].reshape(TOKENS, WIDTH)
-    grad_att[...] = nt(upstream_t, wo_t[...]).astype(BF)
+        grad_att[st * SEQ : st * SEQ + SEQ] = nt(
+            ups_t[st].reshape(SEQ, WIDTH), wo_t[...]
+        ).astype(BF)
+
+    for k in range(3, 6):
+        loads[k].wait()
+    take_cot(0)
     acted_t[0] = acted[0].T.reshape(4, 2, 64, TOKENS)
     att_t[0] = attended[0].T.reshape(4, 2, 64, TOKENS)
 
@@ -303,8 +321,11 @@
         put_rows(joined_t, part, nn(acted_value, wq_t[...]).astype(BF))
 
     for seq in range(2):
+        if seq == 1:
+            take_cot(1)
         for pair in range(PAIRS):
             backward_step(seq, pair, joined_t, None, attended.at[1], grad_att, grad_joined)
+    upstream_t = ups_t[...].reshape(TOKENS, WIDTH)
     gain_sum_t = None
     for part in range(2):
         x_value = part_rows(xt, part)
@@ -552,8 +573,10 @@
         value = value + gain_z_recv[j]
     gains_ref[...] = value
 
-    sent(in_send.at[pl.ds(0, 7)], R_IN)
-    sent(cot_recv.at[:, pl.ds(0, 15)], R_COT)
+    for e in range(2):
+        sent(in_send.at[pl.ds(0, 7), e], R_INS[e])
+    for st in range(2):
+        sent(cot_recv.at[st, pl.ds(0, 15)], R_COTS[st])
     for part in range(2):
         sent(mid_send.at[part, pl.ds(0, 63 + part)], R_MID + part)
         sent(gmid_send.at[part, pl.ds(0, 63 + part)], R_GMID + part)

time: 91.7 us -> 94.1 us (1.026)
  Pallas kernels: 90.9 us -> 93.3 us
    pallas_call x1, Pallas kernels: 89 us -> 91.4 us  [local(): pl.pallas_call(kernel, out_shape=(shape((32, 16, WIDTH), BF), shape((2, 6...]
where the time goes in v5:
time: 94.1 us; the launch traced here: 94 us
  Pallas kernels  93.3 us (99%)
    pallas_call x1, Pallas kernels, local(): pl.pallas_call(kernel, out_shape=(shape((32, 16, WIDTH), BF), shape((2, 6...  91.4 us
    pallas_call x1, Pallas kernels, local(): pl.pallas_call(deliver, out_shape=(shape((32, 16, WIDTH), BF), shape((64,...  1.91 us

profile of v5, /device:TPU:6, one launch (start us, length us, event | category | flops | bytes accessed | tf_op | source)
XLA Modules:
  0.0 94.0 jit_solution(1709493264547608780)
XLA Ops:
  0.6 91.4 %shard_map.135 = (bf16[32,16,512]{2,1,0:T(8,128)(2,1)}, bf16[2,64,128]{2,1,0:T(8,128)(2,1)}, f32[8,128]{1,0:T(8,128)}) custom-call(bf16[32,16,512]{2,1,0:T(8,128)(2,1)} %bitcast.9, bf16[32,16,512]{2,1,0:T(8,128)(2,1)} %bitcast.10, f32[1,512]{1,0:T(1,128)} %bitcast.11, bf16[512,1536]{1,0:T(8,128)(2,1)} %wq_s_hbm.1, bf16[512,512]{1,0:T(8,128)(2,1)} %wo_s_hbm.1, ...), custom_call_target="tpu_custom_call" | custom-call | tf_op jit(solution)/shard_map/pallas_call | solution.py:613
  92.0 1.9 %shard_map.136 = (bf16[32,16,512]{2,1,0:T(8,128)(2,1)}, bf16[64,96]{1,0:T(8,128)(2,1)}, bf16[32,64]{1,0:T(8,128)(2,1)}, f32[1,512]{1,0:T(1,128)}, bf16[64,96]{1,...) custom-call(bf16[32,16,512]{2,1,0:T(8,128)(2,1)} %get-tuple-element.17.gin, ...), custom_call_target="tpu_custom_call" | custom-call | tf_op jit(solution)/shard_map/pallas_call | solution.py:676
